TPU v7x, 512 devices: a whole 4x8x8 slice. The times are simulated.
512 devices in a mesh: rep: 32 (over z_lo, y), fsdp: 16 (over z_hi, x, core).
Axes of the slice: x: 4, y: 8, z: 8 (z_hi: 2, z_lo: 4; z = z_hi * 4 + z_lo), core: 2. Of those that a mesh axis runs over, the one named last changes fastest.
Arguments:
- inputs: bfloat16 [32, 2048, 4096], P('rep', 'fsdp'), may hold values from -6 to 6
- key_grads: bfloat16 [32, 2048, 512], P('rep', 'fsdp'), may hold values from -0.3125 to 0.3125
- weights: float32 [32, 4096, 512], P('rep', 'fsdp'), may hold values from -0.09375 to 0.09375
- first_moment: bfloat16 [32, 4096, 512], P('rep', 'fsdp'), may hold values from -1.25 to 1.25
- second_moment: bfloat16 [32, 4096, 512], P('rep', 'fsdp'), may hold values from 0.099609375 to 1
- drift: float32 [32, 4096, 512], P('rep', 'fsdp'), may hold values from -0.125 to 0.125
- momentum: float32 [4096, 512], P(('fsdp', 'rep')), may hold values from -0.0625 to 0.0625
- global_weights: float32 [4096, 512], P(('fsdp', 'rep')), may hold values from -0.09375 to 0.09375
Outputs:
- keys: bfloat16 [32, 2048, 512], P('rep', 'fsdp')
- input_grads: bfloat16 [32, 2048, 4096], P('rep', 'fsdp')
- merged_weights: float32 [32, 4096, 512], P('rep', 'fsdp')
- new_first_moment: bfloat16 [32, 4096, 512], P('rep', 'fsdp')
- new_second_moment: bfloat16 [32, 4096, 512], P('rep', 'fsdp')
- new_momentum: float32 [4096, 512], P(('fsdp', 'rep'))
- new_global: float32 [4096, 512], P(('fsdp', 'rep'))
All inputs are finite; a program needn't handle non-finite values.
Results may differ from a plain program's by a relative error of at most 0.02.
Values may be sent and summed in bfloat16 or wider, within the bound.
A program may use at most 64 MiB of HBM per device.

v0:
```python
import jax
import jax.numpy as jnp
from jax import lax
from jax.sharding import PartitionSpec as P

HEAD = 128
SEQ = 1024


learning_rate = 0.002
beta_one = 0.9
beta_two = 0.95
adam_epsilon = 1e-08
weight_decay = 0.1
outer_rate = 0.7
outer_beta = 0.9
mixing = 0.5
rope_base = 500000.0


def rope_tables(positions):
    half_size = HEAD // 2
    exponents = jnp.arange(half_size, dtype=jnp.float32) * (2.0 / HEAD)
    inverse_freq = jnp.power(jnp.float32(rope_base), -exponents)
    angles = positions[:, None] * inverse_freq[None, :]
    return (jnp.cos(angles)[:, None, :], jnp.sin(angles)[:, None, :])


def rotate(values, cosine, sines, sign):
    shape = values.shape
    heads = values.reshape(shape[0], shape[1] // HEAD, HEAD)
    half_size = HEAD // 2
    first = heads[..., :half_size]
    second = heads[..., half_size:]
    out_first = first * cosine - sign * second * sines
    out_second = second * cosine + sign * first * sines
    return jnp.concatenate([out_first, out_second], axis=-1).reshape(shape)


def body(inputs, key_grads, weights, first_moment, second_moment, drift, momentum, global_weights):
    tokens = inputs[0]
    master = weights[0]
    token_count = tokens.shape[0]
    first_row = lax.axis_index("fsdp") * token_count
    positions = ((first_row + jnp.arange(token_count, dtype=jnp.int32)) % SEQ).astype(jnp.float32)
    cosine, sines = rope_tables(positions)
    low = master.astype(jnp.bfloat16)
    unrotated = rotate(key_grads[0].astype(jnp.float32), cosine, sines, -1.0).astype(jnp.bfloat16)
    gathered = lax.all_gather(low, "fsdp", axis=0, tiled=True)
    projected = jnp.dot(tokens, gathered, preferred_element_type=jnp.float32)
    backward = lax.dot_general(
        unrotated, gathered, (((1,), (1,)), ((), ())), preferred_element_type=jnp.float32
    )
    rotated = rotate(projected, cosine, sines, 1.0).astype(jnp.bfloat16)
    input_grads = backward.astype(jnp.bfloat16)
    gradient = lax.psum_scatter(
        lax.dot_general(
            tokens, unrotated, (((0,), (0,)), ((), ())), preferred_element_type=jnp.float32
        ).astype(jnp.bfloat16),
        "fsdp",
        scatter_dimension=0,
        tiled=True,
    ).astype(jnp.float32)
    delta = drift[0]
    replicas = lax.axis_size("rep")
    total = lax.psum(delta, "rep")
    mean_drift = total / replicas
    moment_all, global_all = (
        lax.all_gather(momentum, "rep", axis=0, tiled=True),
        lax.all_gather(global_weights, "rep", axis=0, tiled=True),
    )
    moment_next = outer_beta * moment_all + mean_drift
    global_next = global_all - outer_rate * (mean_drift + outer_beta * moment_next)
    piece_rows = momentum.shape[0]
    offset = lax.axis_index("rep") * piece_rows
    new_momentum = lax.dynamic_slice_in_dim(moment_next, offset, piece_rows, 0)
    new_global = lax.dynamic_slice_in_dim(global_next, offset, piece_rows, 0)
    moment_one = beta_one * first_moment[0].astype(jnp.float32) + (1.0 - beta_one) * gradient
    moment_two = (
        beta_two * second_moment[0].astype(jnp.float32) + (1.0 - beta_two) * gradient * gradient
    )
    stepped = master - learning_rate * (
        moment_one / (jnp.sqrt(moment_two) + adam_epsilon) + weight_decay * master
    )
    merged = mixing * stepped + (1.0 - mixing) * global_next
    first_out = moment_one.astype(jnp.bfloat16)
    second_out = moment_two.astype(jnp.bfloat16)
    return (
        rotated[None],
        input_grads[None],
        merged[None],
        first_out[None],
        second_out[None],
        new_momentum,
        new_global,
    )


def solution(mesh):
    placed = (
        P("rep", "fsdp", None),
        P("rep", "fsdp", None),
        P("rep", "fsdp", None),
        P("rep", "fsdp", None),
        P("rep", "fsdp", None),
        P("rep", "fsdp", None),
        P(("fsdp", "rep"), None),
        P(("fsdp", "rep"), None),
    )
    return jax.shard_map(
        body,
        mesh=mesh,
        in_specs=placed,
        out_specs=(
            P("rep", "fsdp", None),
            P("rep", "fsdp", None),
            P("rep", "fsdp", None),
            P("rep", "fsdp", None),
            P("rep", "fsdp", None),
            P(("fsdp", "rep"), None),
            P(("fsdp", "rep"), None),
        ),
        check_vma=False,
    )
```

profile of v0, /device:TPU:2, one launch (start us, length us, event | category | flops | bytes accessed | tf_op | source)
XLA Modules:
  0.0 350.8 jit_solution(15305005040422864944)
XLA Ops:
  8.0 0.0 copy-start
  8.0 0.0 all-reduce.2.cloned.1.call-start
  8.1 2.1 copy.32
  10.2 0.0 all-reduce.2.cloned.1.call-update
  10.2 0.0 reduce-scatter.2.cloned.1.call-start
  10.3 1.0 copy.29
  11.3 0.8 broadcast_multiply_fusion
  12.1 0.0 copy-start.2
  12.2 0.6 copy-done.2
  12.7 0.0 copy-done
  12.8 0.0 copy-start.1
  12.8 3.2 fusion
  16.0 0.0 copy-start.4
  16.0 0.0 copy-start.5
  16.0 0.0 copy-start.7
  16.0 0.0 copy-start.8
  16.0 0.0 reduce-scatter.2.cloned.1.call-update
  16.0 0.0 all-gather.2.cloned.1.call-start
  16.1 0.0 copy-done.1
  16.1 0.2 copy.28
  16.3 0.7 bitcast_convert_fusion
  17.0 0.0 all-gather.2.cloned.1.call-update
  17.1 0.0 copy-done.4
  17.1 0.1 copy.30
  17.2 0.0 copy-done.5
  17.2 0.8 copy.31
  18.1 0.0 copy-done.7
  18.1 85.6 %all_gather.10 = f32[256,512]{1,0:T(8,128)S(1)} all-gather(f32[8,512]{1,0:T(8,128)S(1)} %copy-done.7), channel_id=1, replica_groups=mesh['rep'=32,'fsdp'=16] {'rep'}, dimensions={0}, use_global_device_ids=true | all-gather | bytes 540672 | tf_op jit(solution)/shard_map/all_gather | solution.py:70
  103.6 0.2 copy.34
  103.8 0.0 copy-done.8
  103.8 76.7 %all_gather.11 = f32[256,512]{1,0:T(8,128)S(1)} all-gather(f32[8,512]{1,0:T(8,128)S(1)} %copy-done.8), channel_id=1, replica_groups=mesh['rep'=32,'fsdp'=16] {'rep'}, dimensions={0}, use_global_device_ids=true | all-gather | bytes 540672 | tf_op jit(solution)/shard_map/all_gather | solution.py:69
  180.5 0.2 copy.33
  180.7 144.6 %all-reduce.2.cloned.1.call-done = f32[256,512]{0,1:T(8,128)} async-done(((f32[256,512]{0,1:T(8,128)}), f32[256,512]{0,1:T(8,128)}) %all-reduce.2.cloned.1.call-update) | async-done | bytes 524304 | tf_op jit(solution)/shard_map/psum | solution.py:66
  325.3 0.0 reduce-scatter.2.cloned.1.call-done
  325.3 2.6 fusion.11
  327.9 1.0 copy.36
  328.9 0.0 copy-start.3
  328.9 0.0 copy-start.6
  328.9 1.8 copy.37
  330.7 1.8 copy.38
  332.5 1.2 constant_dynamic-slice_fusion
  333.8 0.7 copy.39
  334.5 0.7 copy.40
  335.2 0.0 all-gather.2.cloned.1.call-done
  335.2 3.4 fusion.2
  338.6 0.0 copy-done.3
  338.6 0.0 copy-done.6
  338.7 0.8 copy.35
  339.5 3.9 %fusion.1 = bf16[1,128,4096]{2,1,0:T(8,128)(2,1)} fusion(bf16[128,512]{0,1:T(8,128)(2,1)S(1)} %bitcast.62, bf16[4096,512]{0,1:T(8,128)(2,1)} %all-gather.2.cloned.1.call-done), kind=kOutput, calls=%fused_computation.3 | convolution fusion | flops 537395200 | bytes 5373952 | tf_op jit(solution)/shard_map/dot_general | solution.py:51
  (6 shorter events, 0.1 us)
Async XLA Ops:
  8.0 4.7 %copy-start = (bf16[1,128,4096]{2,1,0:T(8,128)(2,1)S(1)}, bf16[1,128,4096]{2,1,0:T(8,128)(2,1)}, u32[]{:S(2)}) copy-start(bf16[1,128,4096]{2,1,0:T(8,128)(2,1)} %param.8) | copy-start | bytes 3145732
  8.0 317.3 %all-reduce.2.cloned.1.call-start = ((), (), s32[]{:S(2)}) async-start(), calls=%async_computation.3 | async-start | bytes 1048576 | tf_op jit(solution)/shard_map/psum | solution.py:66
  10.2 315.1 %reduce-scatter.2.cloned.1.call-start = ((), (), s32[]{:S(2)}) async-start(), calls=%async_computation.2 | async-start | bytes 4456448 | tf_op jit(solution)/shard_map/reduce_scatter | solution.py:56
  12.1 0.6 copy-start.2
  12.8 3.3 copy-start.1
  16.0 1.1 copy-start.4
  16.0 1.2 copy-start.5
  16.0 2.1 copy-start.7
  16.0 87.8 %copy-start.8 = (f32[8,512]{1,0:T(8,128)S(1)}, f32[8,512]{1,0:T(8,128)}, u32[]{:S(2)}) copy-start(f32[8,512]{1,0:T(8,128)} %param.14) | copy-start | bytes 49156
  16.0 319.2 %all-gather.2.cloned.1.call-start = ((), (), s32[]{:S(2)}) async-start(), calls=%async_computation.1 | async-start | bytes 4456448 | tf_op jit(solution)/shard_map/all_gather | solution.py:49
  328.9 9.7 %copy-start.3 = (f32[128,64]{0,1:T(8,128)S(1)}, f32[128,64]{0,1:T(8,128)}, u32[]{:S(2)}) copy-start(f32[128,64]{0,1:T(8,128)} %copy-done.2) | copy-start | bytes 98308
  328.9 9.7 %copy-start.6 = (f32[128,64]{0,1:T(8,128)S(1)}, f32[128,64]{0,1:T(8,128)}, u32[]{:S(2)}) copy-start(f32[128,64]{0,1:T(8,128)} %get-tuple-element.31) | copy-start | bytes 98308
Sparse Core Ops, SparseCore 0:
  12.6 312.7 all-reduce.1
Sparse Core Ops, SparseCore 1:
  16.1 120.3 reduce-scatter.1
  140.0 78.3 all-gather.1
where the time goes:
time: 351 us
  blocking collectives  162 us (46%)
  waiting for transfers between devices  145 us (41%)
  between operations  15.7 us (4%)
  local copies, waits for them, and re-layouts  13.3 us (4%)
  matrix products  10.6 us (3%)
  other arithmetic  4.29 us (1%)
    psum x1, waiting for transfers between devices, body(): total = lax.psum(delta, 'rep')  145 us
    all_gather x1, blocking collectives, body(): lax.all_gather(global_weights, 'rep', axis=0, tiled=True)  85.6 us
    all_gather x1, blocking collectives, body(): lax.all_gather(momentum, 'rep', axis=0, tiled=True)  76.7 us
    unnamed x28, local copies, waits for them, and re-layouts  10.7 us
  transfers between devices with their start and end apart: 3, of which 1 were waited for; matrix products, arithmetic and copies ran while one was open for 5% of the time, Pallas kernels for 0%

commit v1 on v0

v1 whole, which is shorter than its diff:
```python
import functools

import jax
import jax.numpy as jnp
import numpy as np
from jax import lax
from jax.experimental import pallas as pl
from jax.experimental.pallas import tpu as pltpu
from jax.sharding import PartitionSpec as P

HEAD = 128
SEQ = 1024
TOK = 128
ROWS = 256
COLS = 512
WIN = 4096
N_REP = 32
N_X = 4
N_Y = 8
N_ZL = 4

learning_rate = 0.002
beta_one = 0.9
beta_two = 0.95
adam_epsilon = 1e-08
weight_decay = 0.1
outer_rate = 0.7
outer_beta = 0.9
mixing = 0.5
rope_base = 500000.0

F32 = jnp.float32
BF16 = jnp.bfloat16
MESH = pl.DeviceIdType.MESH


def rotary_tables():
    half = HEAD // 2
    freq = rope_base ** (-np.arange(half, dtype=np.float64) * (2.0 / HEAD))
    angles = np.arange(SEQ, dtype=np.float64)[:, None] * freq[None, :]
    cosine, sines = np.cos(angles), np.sin(angles)
    first = np.concatenate([cosine, cosine], axis=1)
    second = np.concatenate([-sines, sines], axis=1)
    both = np.stack([first, second]).astype(np.float32)
    return both.reshape(2, SEQ // TOK, TOK, HEAD).transpose(1, 0, 2, 3).copy()


def rotated_heads(values, tables, sign):
    cosine = tables[0]
    sines = sign * tables[1]
    heads = []
    for head in range(COLS // HEAD):
        part = values[:, head * HEAD : (head + 1) * HEAD]
        heads.append(part * cosine + pltpu.roll(part, HEAD // 2, 1) * sines)
    return jnp.concatenate(heads, axis=1)


REMOTE = (
    ("u", 3), ("ap", 3), ("ao", 3), ("igo", 3), ("igp", 3), ("pk", 3),
    ("wsib", 1), ("wz", 1), ("wfwd", 1), ("gpsib", 1), ("gosib", 1), ("gz", 1),
    ("dy", 7), ("dz", 3), ("az", 3), ("ay", 7),
)
LOCAL = (
    "kg", "tab", "w", "m1", "m2", "mo", "gl", "ap", "ao", "dr",
    "igo", "igp", "mg", "m1o", "m2o", "nm", "ng", "keys",
)
FIRST = {}
N_REMOTE = 0
for _name, _count in REMOTE:
    FIRST[_name] = N_REMOTE
    N_REMOTE += _count


def kernel(
    inp, kg, wt, m1, m2, dr, mo, gl, tab,
    keys_out, ig_out, mg_out, m1_out, m2_out, nm_out, ng_out,
    kg_v, tab_v, w_v, m1_v, m2_v, mo_v, gl_v,
    u_all, ap, ao, w_o, w_p, ig_o, ig_p, pk_send, pk_recv, pk_own,
    gp, go, gp_send, gp_recv, go_send, go_recv, gz_send, gz_recv,
    dr_all, ds, dz, ga, gg, nm_v, mg_v, m1o_v, m2o_v, keys_v,
    send_sem, recv_sem, local_sem,
):
    rep = lax.axis_index("rep")
    fsdp = lax.axis_index("fsdp")
    zl, y = rep // N_Y, rep % N_Y
    zh, x, core = fsdp // 8, (fsdp // 2) % N_X, fsdp % 2

    def at_x(step):
        return (rep, zh * 8 + ((x + step) % N_X) * 2 + core)

    def at_y(step):
        return (zl * N_Y + (y + step) % N_Y, fsdp)

    def at_zl(step):
        return (((zl + step) % N_ZL) * N_Y + y, fsdp)

    sibling = (rep, zh * 8 + x * 2 + (1 - core))
    partner = (rep, (1 - zh) * 8 + x * 2 + core)

    def remote(name, index, src, dst, device):
        at = FIRST[name] + index
        return pltpu.make_async_remote_copy(
            src_ref=src, dst_ref=dst, send_sem=send_sem.at[at], recv_sem=recv_sem.at[at],
            device_id=device, device_id_type=MESH,
        )

    def local(name, src, dst):
        return pltpu.make_async_copy(src, dst, local_sem.at[LOCAL.index(name)])

    barrier = pltpu.get_barrier_semaphore()
    peers = [sibling, partner] + [at_x(d) for d in (1, 2, 3)]
    peers += [at_y(e) for e in range(1, N_Y)] + [at_zl(f) for f in range(1, N_ZL)]
    for device in peers:
        pl.semaphore_signal(barrier, inc=1, device_id=device, device_id_type=MESH)

    own_rows = pl.ds(core * ROWS, ROWS)
    sib_rows = pl.ds((1 - core) * ROWS, ROWS)

    def columns(half, chip):
        return pl.ds(pl.multiple_of(half * (WIN // 2) + chip * COLS, COLS), COLS)

    def slot(d):
        return pl.ds(d * TOK, TOK)

    loads = {
        "kg": local("kg", kg.at[0], kg_v),
        "tab": local("tab", tab.at[fsdp % 8], tab_v),
        "w": local("w", wt.at[0], w_v),
        "ap": local("ap", inp.at[0, :, columns(1 - zh, x)], ap.at[slot(0)]),
        "ao": local("ao", inp.at[0, :, columns(zh, x)], ao.at[slot(0)]),
        "dr": local("dr", dr.at[:, y], dr_all.at[0]),
        "m1": local("m1", m1.at[0], m1_v),
        "m2": local("m2", m2.at[0], m2_v),
        "mo": local("mo", mo, mo_v),
        "gl": local("gl", gl, gl_v),
    }
    for copy in loads.values():
        copy.start()

    loads["kg"].wait()
    loads["tab"].wait()
    tables = (tab_v[0], tab_v[1])
    u_all[slot(0), :] = rotated_heads(kg_v[...].astype(F32), tables, -1.0).astype(BF16)
    loads["w"].wait()
    w_o[own_rows, :] = w_v[...].astype(BF16)

    pl.semaphore_wait(barrier, len(peers))

    wz = remote("wz", 0, w_o.at[own_rows], w_p.at[own_rows], partner)
    wsib = remote("wsib", 0, w_o.at[own_rows], w_o.at[own_rows], sibling)
    wz.start()
    wsib.start()
    xs = (1, 3, 2)
    u_copy = {d: remote("u", d - 1, u_all.at[slot(0)], u_all.at[slot(d)], at_x(d)) for d in xs}
    ap_copy = {
        d: remote("ap", d - 1, inp.at[0, :, columns(1 - zh, (x + d) % N_X)], ap.at[slot(d)], at_x(d))
        for d in xs
    }
    ao_copy = {
        d: remote("ao", d - 1, inp.at[0, :, columns(zh, (x + d) % N_X)], ao.at[slot(d)], at_x(d))
        for d in xs
    }
    dy_copy = {
        e: remote("dy", e - 1, dr.at[:, (y + e) % N_Y], dr_all.at[e], at_y(e))
        for e in range(1, N_Y)
    }
    for copies in (u_copy, ap_copy, dy_copy, ao_copy):
        for copy in copies.values():
            copy.start()

    wsib.wait_recv()
    for copy in u_copy.values():
        copy.wait_recv()
    ig_o[...] = lax.dot_general(
        u_all[...], w_o[...], (((1,), (1,)), ((), ())), preferred_element_type=F32
    ).astype(BF16)
    igo_copy = {
        d: remote("igo", d - 1, ig_o.at[slot(d)], ig_out.at[0, :, columns(zh, x)], at_x(4 - d))
        for d in xs
    }
    for copy in igo_copy.values():
        copy.start()
    outs = [local("igo", ig_o.at[slot(0)], ig_out.at[0, :, columns(zh, x)])]
    outs[0].start()

    loads["dr"].wait()
    for copy in dy_copy.values():
        copy.wait_recv()
    total = dr_all[0]
    for e in range(1, N_Y):
        total = total + dr_all[e]
    ds[...] = total
    dz_copy = {
        f: remote("dz", f - 1, ds.at[(zl + f) % N_ZL], dz.at[f - 1], at_zl(f))
        for f in range(1, N_ZL)
    }
    for copy in dz_copy.values():
        copy.start()

    loads["ap"].wait()
    for copy in ap_copy.values():
        copy.wait_recv()
    gp[...] = lax.dot_general(
        ap[...], u_all[...], (((0,), (0,)), ((), ())), preferred_element_type=F32
    )
    gp_send[...] = gp[sib_rows, :].astype(BF16)
    gpsib = remote("gpsib", 0, gp_send, gp_recv, sibling)
    gpsib.start()

    wz.wait_recv()
    wfwd = remote("wfwd", 0, w_p.at[own_rows], w_p.at[own_rows], sibling)
    wfwd.start()

    gpsib.wait_recv()
    gz_send[...] = (gp[own_rows, :] + gp_recv[...].astype(F32)).astype(BF16)
    gz = remote("gz", 0, gz_send, gz_recv, partner)
    gz.start()

    wfwd.wait_recv()
    ig_p[...] = lax.dot_general(
        u_all[...], w_p[...], (((1,), (1,)), ((), ())), preferred_element_type=F32
    ).astype(BF16)
    igp_copy = {
        d: remote("igp", d - 1, ig_p.at[slot(d)], ig_out.at[0, :, columns(1 - zh, x)], at_x(4 - d))
        for d in xs
    }
    for copy in igp_copy.values():
        copy.start()
    outs.append(local("igp", ig_p.at[slot(0)], ig_out.at[0, :, columns(1 - zh, x)]))
    outs[-1].start()

    loads["mo"].wait()
    loads["gl"].wait()
    for copy in dz_copy.values():
        copy.wait_recv()
    mean_drift = (ds[zl] + dz[0] + dz[1] + dz[2]) / N_REP
    moment = outer_beta * mo_v[...] + mean_drift
    nm_v[...] = moment
    ga[zl] = gl_v[...] - outer_rate * (mean_drift + outer_beta * moment)
    az_copy = {
        f: remote("az", f - 1, ga.at[zl], ga.at[zl], at_zl(f)) for f in range(1, N_ZL)
    }
    for copy in az_copy.values():
        copy.start()
    outs.append(local("nm", nm_v, nm_out))
    outs[-1].start()
    outs.append(local("ng", ga.at[zl], ng_out))
    outs[-1].start()

    loads["ao"].wait()
    for copy in ao_copy.values():
        copy.wait_recv()
    for d in (1, 3, 2, 0):
        part = jnp.dot(ao[slot(d), :], w_o[...], preferred_element_type=F32)
        part += jnp.dot(ap[slot(d), :], w_p[...], preferred_element_type=F32)
        if d == 0:
            pk_own[...] = part
        else:
            pk_send[d - 1] = part.astype(BF16)
    pk_copy = {
        d: remote("pk", d - 1, pk_send.at[d - 1], pk_recv.at[d - 1], at_x(4 - d)) for d in xs
    }
    for copy in pk_copy.values():
        copy.start()

    for copy in az_copy.values():
        copy.wait_recv()
    ay_copy = {
        e: remote("ay", e - 1, ga, gg.at[:, y], at_y(e)) for e in range(1, N_Y)
    }
    for copy in ay_copy.values():
        copy.start()
    gg[:, y] = ga[...]

    go[...] = lax.dot_general(
        ao[...], u_all[...], (((0,), (0,)), ((), ())), preferred_element_type=F32
    )
    go_send[...] = go[sib_rows, :].astype(BF16)
    gosib = remote("gosib", 0, go_send, go_recv, sibling)
    gosib.start()

    loads["m1"].wait()
    loads["m2"].wait()
    gosib.wait_recv()
    for copy in ay_copy.values():
        copy.wait_recv()
    gz.wait_recv()

    own = core * ROWS
    for zone in range(N_ZL):
        rows = pl.ds(zone * 64, 64)
        gradient = (
            go[pl.ds(own + zone * 64, 64), :]
            + go_recv[rows, :].astype(F32)
            + gz_recv[rows, :].astype(F32)
        )
        master = w_v[rows, :]
        moment_one = beta_one * m1_v[rows, :].astype(F32) + (1.0 - beta_one) * gradient
        moment_two = (
            beta_two * m2_v[rows, :].astype(F32) + (1.0 - beta_two) * gradient * gradient
        )
        stepped = master - learning_rate * (
            moment_one / (jnp.sqrt(moment_two) + adam_epsilon) + weight_decay * master
        )
        mg_v[rows, :] = mixing * stepped + (1.0 - mixing) * gg[zone].reshape(64, COLS)
        m1o_v[rows, :] = moment_one.astype(BF16)
        m2o_v[rows, :] = moment_two.astype(BF16)
    for name, src, dst in (("mg", mg_v, mg_out), ("m1o", m1o_v, m1_out), ("m2o", m2o_v, m2_out)):
        outs.append(local(name, src, dst.at[0]))
        outs[-1].start()

    for copy in pk_copy.values():
        copy.wait_recv()
    projected = pk_own[...]
    for d in range(3):
        projected = projected + pk_recv[d].astype(F32)
    keys_v[...] = rotated_heads(projected, tables, 1.0).astype(BF16)
    outs.append(local("keys", keys_v, keys_out.at[0]))
    outs[-1].start()

    for copies in (igo_copy, igp_copy):
        for copy in copies.values():
            copy.wait_recv()
    for copies in (u_copy, ap_copy, ao_copy, dy_copy, igo_copy, igp_copy, dz_copy, az_copy, ay_copy, pk_copy):
        for copy in copies.values():
            copy.wait_send()
    for copy in (wz, wsib, wfwd, gpsib, gosib, gz):
        copy.wait_send()
    for copy in outs:
        copy.wait()


def body(inputs, key_grads, weights, first_moment, second_moment, drift, momentum, global_weights):
    shape = jax.ShapeDtypeStruct
    vmem = pltpu.VMEM
    big = (4 * TOK, COLS)
    piece = (N_ZL, 8, COLS)
    scratch = [
        vmem((TOK, COLS), BF16), vmem((2, TOK, HEAD), F32), vmem((ROWS, COLS), F32),
        vmem((ROWS, COLS), BF16), vmem((ROWS, COLS), BF16), vmem((8, COLS), F32), vmem((8, COLS), F32),
        vmem(big, BF16), vmem(big, BF16), vmem(big, BF16), vmem(big, BF16), vmem(big, BF16),
        vmem(big, BF16), vmem(big, BF16),
        vmem((3, TOK, COLS), BF16), vmem((3, TOK, COLS), BF16), vmem((TOK, COLS), F32),
        vmem(big, F32), vmem(big, F32),
        vmem((ROWS, COLS), BF16), vmem((ROWS, COLS), BF16), vmem((ROWS, COLS), BF16),
        vmem((ROWS, COLS), BF16), vmem((ROWS, COLS), BF16), vmem((ROWS, COLS), BF16),
        vmem((N_Y,) + piece, F32), vmem(piece, F32), vmem((3, 8, COLS), F32), vmem(piece, F32),
        vmem((N_ZL, N_Y, 8, COLS), F32), vmem((8, COLS), F32), vmem((ROWS, COLS), F32),
        vmem((ROWS, COLS), BF16), vmem((ROWS, COLS), BF16), vmem((TOK, COLS), BF16),
        pltpu.SemaphoreType.DMA((N_REMOTE,)), pltpu.SemaphoreType.DMA((N_REMOTE,)),
        pltpu.SemaphoreType.DMA((len(LOCAL),)),
    ]
    outs = (
        shape((1, TOK, COLS), BF16), shape((1, TOK, WIN), BF16), shape((1, ROWS, COLS), F32),
        shape((1, ROWS, COLS), BF16), shape((1, ROWS, COLS), BF16),
        shape((8, COLS), F32), shape((8, COLS), F32),
    )
    anywhere = pl.BlockSpec(memory_space=pl.ANY)
    return pl.pallas_call(
        kernel,
        out_shape=outs,
        in_specs=[anywhere] * 9,
        out_specs=[anywhere] * 7,
        scratch_shapes=scratch,
        compiler_params=pltpu.CompilerParams(
            collective_id=0, has_side_effects=True, vmem_limit_bytes=56 * 2**20
        ),
    )(
        inputs, key_grads, weights, first_moment, second_moment,
        drift.reshape(N_ZL, N_Y, 8, COLS), momentum, global_weights, jnp.asarray(rotary_tables()),
    )


def solution(mesh):
    split = P("rep", "fsdp", None)
    rows = P(("fsdp", "rep"), None)
    return jax.shard_map(
        body,
        mesh=mesh,
        in_specs=(split,) * 6 + (rows,) * 2,
        out_specs=(split,) * 5 + (rows,) * 2,
        check_vma=False,
    )
```

time: 351 us -> 73.1 us (0.21)
  the two profiles are of different devices: /device:TPU:2 before, /device:TPU:1 now
where the time goes in v1:
time: 73.1 us; the launch traced here: 72.7 us
  Pallas kernels  64 us (88%)
  local copies, waits for them, and re-layouts  8.1 us (11%)
    pallas_call x1, Pallas kernels, body(): pl.pallas_call(kernel, out_shape=outs, in_specs=[anywhere] * 9, out_specs...  64 us
    unnamed x17, local copies, waits for them, and re-layouts  8.1 us

profile of v1, /device:TPU:1, one launch (start us, length us, event | category | flops | bytes accessed | tf_op | source)
XLA Modules:
  0.0 72.7 jit_solution(1919689405069128512)
XLA Ops:
  0.6 64.0 %shard_map.144 = (bf16[1,128,512]{2,1,0:T(8,128)(2,1)}, bf16[1,128,4096]{2,1,0:T(8,128)(2,1)}, f32[1,256,512]{2,1,0:T(8,128)}, bf16[1,256,512]{2,1,0:T(8,128)(2,...) custom-call(bf16[1,128,4096]{2,1,0:T(8,128)(2,1)} %inp.1, bf16[1,128,512]{2,1,0:T(8,128)(2,1)} %kg.1, ...), custom_call_target="tpu_custom_call" | custom-call | tf_op jit(solution)/shard_map/pallas_call | solution.py:359
  64.6 1.6 %copy.23 = bf16[1,128,512]{2,1,0:T(8,128)(2,1)} copy(bf16[1,128,512]{2,1,0:T(8,128)(2,1)} %get-tuple-element.14) | data formatting | bytes 262144
  66.2 0.0 copy-start
  66.2 2.3 %copy.24 = bf16[1,128,4096]{2,1,0:T(8,128)(2,1)} copy(bf16[1,128,4096]{2,1,0:T(8,128)(2,1)} %get-tuple-element.15) | data formatting | bytes 2097152
  68.5 0.0 copy-done
  68.5 0.0 copy-start.2
  68.5 0.8 %copy.25 = f32[1,256,512]{2,1,0:T(8,128)} copy(f32[1,256,512]{2,1,0:T(8,128)S(1)} %copy-done) | data formatting | bytes 1048576
  69.3 0.3 copy-done.2
  69.6 0.0 copy-start.1
  69.6 0.7 copy.26
  70.3 0.3 copy-done.1
  70.7 0.0 copy-start.4
  70.7 0.7 copy.27
  71.4 0.0 copy-done.4
  71.4 0.0 copy-start.3
  71.4 0.6 copy.28
  72.0 0.1 copy-done.3
  72.1 0.6 copy.29
Async XLA Ops:
  66.2 2.3 %copy-start = (f32[1,256,512]{2,1,0:T(8,128)S(1)}, f32[1,256,512]{2,1,0:T(8,128)}, u32[]{:S(2)}) copy-start(f32[1,256,512]{2,1,0:T(8,128)} %get-tuple-element.16) | copy-start | bytes 1572868
  68.5 1.1 %copy-start.2 = (bf16[1,256,512]{2,1,0:T(8,128)(2,1)S(1)}, bf16[1,256,512]{2,1,0:T(8,128)(2,1)}, u32[]{:S(2)}) copy-start(bf16[1,256,512]{2,1,0:T(8,128)(2,1)} %get-tuple-element.17) | copy-start | bytes 786436
  69.6 1.0 %copy-start.1 = (bf16[1,256,512]{2,1,0:T(8,128)(2,1)S(1)}, bf16[1,256,512]{2,1,0:T(8,128)(2,1)}, u32[]{:S(2)}) copy-start(bf16[1,256,512]{2,1,0:T(8,128)(2,1)} %get-tuple-element.18) | copy-start | bytes 786436
  70.7 0.7 copy-start.4
  71.4 0.7 copy-start.3

commit v2 on v1

v2 whole, which is shorter than its diff:
```python
import functools

import jax
import jax.numpy as jnp
import numpy as np
from jax import lax
from jax.experimental import pallas as pl
from jax.experimental.pallas import tpu as pltpu
from jax.sharding import PartitionSpec as P

HEAD = 128
SEQ = 1024
TOK = 128
ROWS = 256
COLS = 512
WIN = 4096
N_REP = 32
N_X = 4
N_Y = 8
N_ZL = 4

learning_rate = 0.002
beta_one = 0.9
beta_two = 0.95
adam_epsilon = 1e-08
weight_decay = 0.1
outer_rate = 0.7
outer_beta = 0.9
mixing = 0.5
rope_base = 500000.0

F32 = jnp.float32
BF16 = jnp.bfloat16
MESH = pl.DeviceIdType.MESH


def rotary_tables():
    half = HEAD // 2
    freq = rope_base ** (-np.arange(half, dtype=np.float64) * (2.0 / HEAD))
    angles = np.arange(SEQ, dtype=np.float64)[:, None] * freq[None, :]
    cosine, sines = np.cos(angles), np.sin(angles)
    first = np.concatenate([cosine, cosine], axis=1)
    second = np.concatenate([-sines, sines], axis=1)
    both = np.stack([first, second]).astype(np.float32)
    return both.reshape(2, SEQ // TOK, TOK, HEAD).transpose(1, 0, 2, 3).copy()


def rotated_heads(values, tables, sign):
    cosine = tables[0]
    sines = sign * tables[1]
    heads = []
    for head in range(COLS // HEAD):
        part = values[:, head * HEAD : (head + 1) * HEAD]
        heads.append(part * cosine + pltpu.roll(part, HEAD // 2, 1) * sines)
    return jnp.concatenate(heads, axis=1)


REMOTE = (
    ("u", N_X), ("ap", N_X), ("ao", N_X), ("igo", N_X), ("igp", N_X), ("pk", N_X),
    ("wsib", 1), ("wz", 1), ("wfwd", 1), ("gpsib", 1), ("gosib", 1), ("gz", 1),
    ("dy", 7), ("dz", 3), ("base", 3), ("ay", 7),
)
LOCAL = (
    "kg", "tab", "w", "m1", "m2", "mo", "gl", "ap", "ao", "dr",
    "igo", "igp", "mg", "m1o", "m2o", "nm", "ng", "keys",
)
FIRST = {}
N_REMOTE = 0
for _name, _count in REMOTE:
    FIRST[_name] = N_REMOTE
    N_REMOTE += _count
MET_SIB, MET_Z, MET_Y, MET_ZL = N_X, N_X + 1, N_X + 2, N_X + 3


def kernel(
    inp, kg, wt, m1, m2, dr, mo, gl, tab,
    keys_out, ig_out, mg_out, m1_out, m2_out, nm_out, ng_out,
    kg_v, tab_v, w_v, m1_v, m2_v, mo_v, gl_v,
    u_all, ap, ao, w_o, w_p, ig_o, ig_p, pk_send, pk_recv, pk_own,
    gp, go, gp_send, gp_recv, go_send, go_recv, gz_send, gz_recv,
    dr_v, dr_low, dr_all, ds, ds_low, dz, base, mean_all, ga_low, gg, nm_v, ng_v, mg_v, m1o_v, m2o_v, keys_v,
    send_sem, recv_sem, local_sem, met,
):
    rep = lax.axis_index("rep")
    fsdp = lax.axis_index("fsdp")
    zl, y = rep // N_Y, rep % N_Y
    zh, x, core = fsdp // 8, (fsdp // 2) % N_X, fsdp % 2

    def chip_x(peer):
        return (rep, zh * 8 + peer * 2 + core)

    def chip_y(peer):
        return (zl * N_Y + peer, fsdp)

    def chip_zl(peer):
        return (peer * N_Y + y, fsdp)

    def at_y(step):
        return chip_y((y + step) % N_Y)

    def at_zl(step):
        return chip_zl((zl + step) % N_ZL)

    sibling = (rep, zh * 8 + x * 2 + (1 - core))
    partner = (rep, (1 - zh) * 8 + x * 2 + core)

    def remote(name, send, recv, src, dst, device):
        return pltpu.make_async_remote_copy(
            src_ref=src, dst_ref=dst, send_sem=send_sem.at[FIRST[name] + send],
            recv_sem=recv_sem.at[FIRST[name] + recv], device_id=device, device_id_type=MESH,
        )

    def local(name, src, dst):
        return pltpu.make_async_copy(src, dst, local_sem.at[LOCAL.index(name)])

    def signal(semaphore, device):
        pl.semaphore_signal(semaphore, inc=1, device_id=device, device_id_type=MESH)

    def wait_for(semaphore, count):
        @pl.when(count > 0)
        def _():
            pl.semaphore_wait(semaphore, count)

    own_rows = pl.ds(pl.multiple_of(core * ROWS, ROWS), ROWS)
    sib_rows = pl.ds(pl.multiple_of((1 - core) * ROWS, ROWS), ROWS)

    def columns(half, chip):
        return pl.ds(pl.multiple_of(half * (WIN // 2) + chip * COLS, COLS), COLS)

    def slot(chip):
        return pl.ds(pl.multiple_of(chip * TOK, TOK), TOK)

    barrier = pltpu.get_barrier_semaphore()
    for peer in range(1, N_X):
        @pl.when(peer > x)
        def _():
            signal(barrier, chip_x(peer))
    for peer in range(1, N_Y):
        @pl.when(peer > y)
        def _():
            signal(barrier, chip_y(peer))
    for peer in range(1, N_ZL):
        @pl.when(peer > zl)
        def _():
            signal(barrier, chip_zl(peer))

    @pl.when(core == 0)
    def _():
        signal(barrier, sibling)

    @pl.when(zh == 0)
    def _():
        signal(barrier, partner)

    loads = {
        "kg": local("kg", kg.at[0], kg_v),
        "tab": local("tab", tab.at[fsdp % 8], tab_v),
        "w": local("w", wt.at[0], w_v),
        "ap": local("ap", inp.at[0, :, columns(1 - zh, x)], ap.at[slot(x)]),
        "ao": local("ao", inp.at[0, :, columns(zh, x)], ao.at[slot(x)]),
        "dr": local("dr", dr, dr_v),
        "m1": local("m1", m1.at[0], m1_v),
        "m2": local("m2", m2.at[0], m2_v),
        "mo": local("mo", mo, mo_v),
        "gl": local("gl", gl, gl_v),
    }
    for copy in loads.values():
        copy.start()

    loads["kg"].wait()
    loads["tab"].wait()
    tables = (tab_v[0], tab_v[1])
    u_all[slot(x), :] = rotated_heads(kg_v[...].astype(F32), tables, -1.0).astype(BF16)
    loads["w"].wait()
    w_o[own_rows, :] = w_v[...].astype(BF16)

    loads["dr"].wait()
    for peer in range(N_Y):
        dr_low[peer] = dr_v[:, peer].reshape(N_ZL * 8, COLS).astype(BF16)

    wait_for(barrier, x + y + zl + core + zh)
    for peer in range(N_X - 1):
        @pl.when(peer < x)
        def _():
            signal(met.at[x], chip_x(peer))

    @pl.when(core == 1)
    def _():
        signal(met.at[MET_SIB], sibling)

    @pl.when(zh == 1)
    def _():
        signal(met.at[MET_Z], partner)

    for peer in range(N_Y - 1):
        @pl.when(peer < y)
        def _():
            signal(met.at[MET_Y], chip_y(peer))
    for peer in range(N_ZL - 1):
        @pl.when(peer < zl)
        def _():
            signal(met.at[MET_ZL], chip_zl(peer))

    wz = remote("wz", 0, 0, w_o.at[own_rows], w_p.at[own_rows], partner)
    wsib = remote("wsib", 0, 0, w_o.at[own_rows], w_o.at[own_rows], sibling)

    @pl.when(zh == 1)
    def _():
        wz.start()

    @pl.when(core == 1)
    def _():
        wsib.start()

    def to_x(name, src, dst):
        return [remote(name, peer, x, src(peer), dst(peer), chip_x(peer)) for peer in range(N_X)]

    def each_peer(act):
        for peer in range(N_X):
            pl.when(peer != x)(functools.partial(act, peer))

    def wait_x(name, shape_of):
        def wait(peer):
            remote(name, peer, peer, shape_of, shape_of, chip_x(peer)).wait_recv()

        each_peer(wait)

    tall = u_all.at[slot(0)]
    u_copy = to_x("u", lambda peer: u_all.at[slot(x)], lambda peer: u_all.at[slot(x)])
    ap_copy = to_x(
        "ap", lambda peer: inp.at[0, :, columns(1 - zh, peer)], lambda peer: ap.at[slot(x)]
    )
    ao_copy = to_x(
        "ao", lambda peer: inp.at[0, :, columns(zh, peer)], lambda peer: ao.at[slot(x)]
    )

    def first_sends(peer):
        @pl.when(peer > x)
        def _():
            pl.semaphore_wait(met.at[peer], 1)

        u_copy[peer].start()

    late = (zh == 1) & (core == 1)
    for peer in range(N_X - 1):
        pl.when(peer != x)(functools.partial(first_sends, peer))

    @pl.when((x != N_X - 1) & jnp.logical_not(late))
    def _():
        first_sends(N_X - 1)

    for peer in range(N_X):
        pl.when((peer != x) & ((peer < N_X - 1) | jnp.logical_not(late)))(ap_copy[peer].start)

    dy_copy = [
        remote("dy", e - 1, e - 1, dr_low.at[(y + e) % N_Y], dr_all.at[e - 1], at_y(e))
        for e in range(1, N_Y)
    ]
    wait_for(met.at[MET_Y], N_Y - 1 - y)
    for copy in dy_copy:
        copy.start()

    @pl.when((x != N_X - 1) & late)
    def _():
        first_sends(N_X - 1)
        ap_copy[N_X - 1].start()

    @pl.when(core == 0)
    def _():
        pl.semaphore_wait(met.at[MET_SIB], 1)
        wsib.start()

    each_peer(lambda peer: ao_copy[peer].start())

    @pl.when(zh == 0)
    def _():
        pl.semaphore_wait(met.at[MET_Z], 1)
        wz.start()

    wsib.wait_recv()
    wait_x("u", tall)
    ig_o[...] = lax.dot_general(
        u_all[...], w_o[...], (((1,), (1,)), ((), ())), preferred_element_type=F32
    ).astype(BF16)
    igo_copy = to_x(
        "igo", lambda peer: ig_o.at[slot(peer)], lambda peer: ig_out.at[0, :, columns(zh, x)]
    )
    each_peer(lambda peer: igo_copy[peer].start())
    outs = [local("igo", ig_o.at[slot(x)], ig_out.at[0, :, columns(zh, x)])]
    outs[0].start()

    for copy in dy_copy:
        copy.wait_recv()
    total = dr_v[:, y].reshape(N_ZL * 8, COLS)
    for e in range(N_Y - 1):
        total = total + dr_all[e].astype(F32)
    ds[...] = total
    ds_low[...] = total.astype(BF16)
    loads["mo"].wait()
    loads["gl"].wait()
    base[zl] = gl_v[...] - (outer_rate * outer_beta * outer_beta) * mo_v[...]
    dz_copy = [
        remote("dz", f - 1, f - 1, ds_low, dz.at[f - 1], at_zl(f)) for f in range(1, N_ZL)
    ]
    base_copy = [
        remote("base", f - 1, f - 1, base.at[zl], base.at[zl], at_zl(f)) for f in range(1, N_ZL)
    ]
    wait_for(met.at[MET_ZL], N_ZL - 1 - zl)
    for copy in dz_copy + base_copy:
        copy.start()

    loads["ap"].wait()
    wait_x("ap", tall)
    gp[...] = lax.dot_general(
        ap[...], u_all[...], (((0,), (0,)), ((), ())), preferred_element_type=F32
    )
    gp_send[...] = gp[sib_rows, :].astype(BF16)
    gpsib = remote("gpsib", 0, 0, gp_send, gp_recv, sibling)
    gpsib.start()

    wz.wait_recv()
    wfwd = remote("wfwd", 0, 0, w_p.at[own_rows], w_p.at[own_rows], sibling)
    wfwd.start()
    gpsib.wait_recv()
    gz_send[...] = (gp[own_rows, :] + gp_recv[...].astype(F32)).astype(BF16)
    wfwd.wait_recv()

    ig_p[...] = lax.dot_general(
        u_all[...], w_p[...], (((1,), (1,)), ((), ())), preferred_element_type=F32
    ).astype(BF16)
    igp_copy = to_x(
        "igp", lambda peer: ig_p.at[slot(peer)], lambda peer: ig_out.at[0, :, columns(1 - zh, x)]
    )
    each_peer(lambda peer: igp_copy[peer].start())
    outs.append(local("igp", ig_p.at[slot(x)], ig_out.at[0, :, columns(1 - zh, x)]))
    outs[-1].start()

    for copy in dz_copy + base_copy:
        copy.wait_recv()
    total = ds[...]
    for step in range(N_ZL - 1):
        total = total + dz[step].astype(F32)
    mean_all[...] = (total / N_REP).reshape(N_ZL, 8, COLS)
    fresh = base[...] - (outer_rate * (1.0 + outer_beta)) * mean_all[...]
    ga_low[...] = fresh.reshape(N_ZL * 8, COLS).astype(BF16)
    ay_copy = [remote("ay", e - 1, e - 1, ga_low, gg.at[y], at_y(e)) for e in range(1, N_Y)]
    for copy in ay_copy:
        copy.start()
    gg[y] = ga_low[...]
    mean_drift = mean_all[zl]
    moment = outer_beta * mo_v[...] + mean_drift
    nm_v[...] = moment
    ng_v[...] = gl_v[...] - outer_rate * (mean_drift + outer_beta * moment)
    outs.append(local("nm", nm_v, nm_out))
    outs[-1].start()
    outs.append(local("ng", ng_v, ng_out))
    outs[-1].start()

    gz = remote("gz", 0, 0, gz_send, gz_recv, partner)
    gz.start()

    loads["ao"].wait()
    wait_x("ao", tall)
    go[...] = lax.dot_general(
        ao[...], u_all[...], (((0,), (0,)), ((), ())), preferred_element_type=F32
    )
    go_send[...] = go[sib_rows, :].astype(BF16)
    gosib = remote("gosib", 0, 0, go_send, go_recv, sibling)
    gosib.start()

    pk_copy = to_x("pk", lambda peer: pk_send.at[peer], lambda peer: pk_recv.at[(peer - x + 3) % 4])
    for peer in range(N_X):
        part = jnp.dot(ao[slot(peer), :], w_o[...], preferred_element_type=F32)
        part += jnp.dot(ap[slot(peer), :], w_p[...], preferred_element_type=F32)

        @pl.when(peer == x)
        def _():
            pk_own[...] = part

        @pl.when(peer != x)
        def _():
            pk_send[peer] = part.astype(BF16)
            pk_copy[peer].start()

    loads["m1"].wait()
    loads["m2"].wait()
    gosib.wait_recv()
    for copy in ay_copy:
        copy.wait_recv()
    gz.wait_recv()

    for zone in range(N_ZL):
        rows = pl.ds(zone * 64, 64)
        gradient = (
            go[pl.ds(pl.multiple_of(core * ROWS + zone * 64, 64), 64), :]
            + go_recv[rows, :].astype(F32)
            + gz_recv[rows, :].astype(F32)
        )
        master = w_v[rows, :]
        spread = gg[:, pl.ds(zone * 8, 8), :].astype(F32).reshape(64, COLS)
        moment_one = beta_one * m1_v[rows, :].astype(F32) + (1.0 - beta_one) * gradient
        moment_two = (
            beta_two * m2_v[rows, :].astype(F32) + (1.0 - beta_two) * gradient * gradient
        )
        stepped = master - learning_rate * (
            moment_one / (jnp.sqrt(moment_two) + adam_epsilon) + weight_decay * master
        )
        mg_v[rows, :] = mixing * stepped + (1.0 - mixing) * spread
        m1o_v[rows, :] = moment_one.astype(BF16)
        m2o_v[rows, :] = moment_two.astype(BF16)
    for name, src, dst in (("mg", mg_v, mg_out), ("m1o", m1o_v, m1_out), ("m2o", m2o_v, m2_out)):
        outs.append(local(name, src, dst.at[0]))
        outs[-1].start()

    wait_x("pk", tall)
    projected = pk_own[...]
    for step in range(3):
        projected = projected + pk_recv[step].astype(F32)
    keys_v[...] = rotated_heads(projected, tables, 1.0).astype(BF16)
    outs.append(local("keys", keys_v, keys_out.at[0]))
    outs[-1].start()

    wait_x("igo", tall)
    wait_x("igp", tall)
    for copies in (u_copy, ap_copy, ao_copy, igo_copy, igp_copy, pk_copy):
        each_peer(lambda peer: copies[peer].wait_send())
    for copy in dy_copy + dz_copy + base_copy + ay_copy + [wz, wsib, wfwd, gpsib, gosib, gz]:
        copy.wait_send()
    for copy in outs:
        copy.wait()


PIECES = ((1, 32), (1, 32), (1, 32), (1, 32), (2, 128), (2, 128), (3, 256), (4, 256), (0, 128), (5, 8), (6, 8))


def hand_over(*refs):
    given, taken, held, sems = refs[:7], refs[7:14], refs[14:21], refs[21]
    loads, stores, done = [], [], [0] * 7
    for at, (which, rows) in enumerate(PIECES):
        src, dst = given[which], taken[which]
        if which < 5:
            src, dst = src.at[0], dst.at[0]
        part = pl.ds(done[which], rows)
        done[which] += rows
        loads.append(pltpu.make_async_copy(src.at[part], held[which].at[part], sems.at[0, at]))
        stores.append(pltpu.make_async_copy(held[which].at[part], dst.at[part], sems.at[1, at]))
    for copy in loads:
        copy.start()
    for load, store in zip(loads, stores):
        load.wait()
        store.start()
    for copy in stores:
        copy.wait()


def body(inputs, key_grads, weights, first_moment, second_moment, drift, momentum, global_weights):
    shape = jax.ShapeDtypeStruct
    vmem = pltpu.VMEM
    big = (4 * TOK, COLS)
    piece = (N_ZL, 8, COLS)
    scratch = [
        vmem((TOK, COLS), BF16), vmem((2, TOK, HEAD), F32), vmem((ROWS, COLS), F32),
        vmem((ROWS, COLS), BF16), vmem((ROWS, COLS), BF16), vmem((8, COLS), F32), vmem((8, COLS), F32),
        vmem(big, BF16), vmem(big, BF16), vmem(big, BF16), vmem(big, BF16), vmem(big, BF16),
        vmem(big, BF16), vmem(big, BF16),
        vmem((N_X, TOK, COLS), BF16), vmem((3, TOK, COLS), BF16), vmem((TOK, COLS), F32),
        vmem(big, F32), vmem(big, F32),
        vmem((ROWS, COLS), BF16), vmem((ROWS, COLS), BF16), vmem((ROWS, COLS), BF16),
        vmem((ROWS, COLS), BF16), vmem((ROWS, COLS), BF16), vmem((ROWS, COLS), BF16),
        vmem((N_ZL, N_Y, 8, COLS), F32), vmem((N_Y, N_ZL * 8, COLS), BF16), vmem((N_Y - 1, N_ZL * 8, COLS), BF16),
        vmem((N_ZL * 8, COLS), F32), vmem((N_ZL * 8, COLS), BF16),
        vmem((3, N_ZL * 8, COLS), BF16), vmem(piece, F32), vmem(piece, F32), vmem((N_ZL * 8, COLS), BF16),
        vmem((N_Y, N_ZL * 8, COLS), BF16), vmem((8, COLS), F32), vmem((8, COLS), F32), vmem((ROWS, COLS), F32),
        vmem((ROWS, COLS), BF16), vmem((ROWS, COLS), BF16), vmem((TOK, COLS), BF16),
        pltpu.SemaphoreType.DMA((N_REMOTE,)), pltpu.SemaphoreType.DMA((N_REMOTE,)),
        pltpu.SemaphoreType.DMA((len(LOCAL),)), pltpu.SemaphoreType.REGULAR((N_X + 4,)),
    ]
    outs = (
        shape((1, TOK, COLS), BF16), shape((1, TOK, WIN), BF16), shape((1, ROWS, COLS), F32),
        shape((1, ROWS, COLS), BF16), shape((1, ROWS, COLS), BF16),
        shape((8, COLS), F32), shape((8, COLS), F32),
    )
    anywhere = pl.BlockSpec(memory_space=pl.ANY)
    results = pl.pallas_call(
        kernel,
        out_shape=outs,
        in_specs=[anywhere] * 9,
        out_specs=[anywhere] * 7,
        scratch_shapes=scratch,
        compiler_params=pltpu.CompilerParams(
            collective_id=0, has_side_effects=True, vmem_limit_bytes=56 * 2**20
        ),
    )(
        inputs, key_grads, weights, first_moment, second_moment,
        drift.reshape(N_ZL, N_Y, 8, COLS), momentum, global_weights, jnp.asarray(rotary_tables()),
    )
    return pl.pallas_call(
        hand_over,
        out_shape=outs,
        in_specs=[anywhere] * 7,
        out_specs=[anywhere] * 7,
        scratch_shapes=[vmem(out.shape[-2:], out.dtype) for out in outs]
        + [pltpu.SemaphoreType.DMA((2, len(PIECES)))],
        compiler_params=pltpu.CompilerParams(vmem_limit_bytes=56 * 2**20),
    )(*results)


def solution(mesh):
    split = P("rep", "fsdp", None)
    rows = P(("fsdp", "rep"), None)
    return jax.shard_map(
        body,
        mesh=mesh,
        in_specs=(split,) * 6 + (rows,) * 2,
        out_specs=(split,) * 5 + (rows,) * 2,
        check_vma=False,
    )
```

time: 73.1 us -> 50.5 us (0.69)
  the two profiles are of different devices: /device:TPU:1 before, /device:TPU:70 now
where the time goes in v2:
time: 50.5 us; the launch traced here: 50.3 us
  Pallas kernels  49.7 us (98%)
  between operations  0.64 us (1%)
    pallas_call x1, Pallas kernels, body(): pl.pallas_call(kernel, out_shape=outs, in_specs=[anywhere] * 9, out_specs...  47.2 us
    pallas_call x1, Pallas kernels, body(): pl.pallas_call(hand_over, out_shape=outs, in_specs=[anywhere] * 7, out_sp...  2.49 us

profile of v2, /device:TPU:70, one launch (start us, length us, event | category | flops | bytes accessed | tf_op | source)
XLA Modules:
  0.0 50.3 jit_solution(17380942043273837674)
XLA Ops:
  0.6 47.2 %shard_map.144 = (bf16[1,128,512]{2,1,0:T(8,128)(2,1)}, bf16[1,128,4096]{2,1,0:T(8,128)(2,1)}, f32[1,256,512]{2,1,0:T(8,128)}, bf16[1,256,512]{2,1,0:T(8,128)(2,...) custom-call(bf16[1,128,4096]{2,1,0:T(8,128)(2,1)} %inp.1, bf16[1,128,512]{2,1,0:T(8,128)(2,1)} %kg.1, ...), custom_call_target="tpu_custom_call" | custom-call | tf_op jit(solution)/shard_map/pallas_call | solution.py:484
  47.8 2.5 %shard_map.145 = (bf16[1,128,512]{2,1,0:T(8,128)(2,1)}, bf16[1,128,4096]{2,1,0:T(8,128)(2,1)}, f32[1,256,512]{2,1,0:T(8,128)}, bf16[1,256,512]{2,1,0:T(8,128)(2,...) custom-call(bf16[1,128,512]{2,1,0:T(8,128)(2,1)} %get-tuple-element.14.refs_0_, ...), custom_call_target="tpu_custom_call" | custom-call | tf_op jit(solution)/shard_map/pallas_call | solution.py:497

commit v3 on v2

--- a/solution.py
+++ b/solution.py
@@ -57,8 +57,8 @@
 
 REMOTE = (
     ("u", N_X), ("ap", N_X), ("ao", N_X), ("igo", N_X), ("igp", N_X), ("pk", N_X),
-    ("wsib", 1), ("wz", 1), ("wfwd", 1), ("gpsib", 1), ("gosib", 1), ("gz", 1),
-    ("dy", 7), ("dz", 3), ("base", 3), ("ay", 7),
+    ("wsib", 1), ("wz", 2), ("wfwd", 2), ("gpsib", 1), ("gosib", 1), ("gz", 1),
+    ("dy", 7), ("dz", 3), ("ay", 7),
 )
 LOCAL = (
     "kg", "tab", "w", "m1", "m2", "mo", "gl", "ap", "ao", "dr",
@@ -78,7 +78,7 @@
     kg_v, tab_v, w_v, m1_v, m2_v, mo_v, gl_v,
     u_all, ap, ao, w_o, w_p, ig_o, ig_p, pk_send, pk_recv, pk_own,
     gp, go, gp_send, gp_recv, go_send, go_recv, gz_send, gz_recv,
-    dr_v, dr_low, dr_all, ds, ds_low, dz, base, mean_all, ga_low, gg, nm_v, ng_v, mg_v, m1o_v, m2o_v, keys_v,
+    dr_v, dr_low, dr_all, ds, with_base, ds_low, dz, dz_wide, ga_low, gg, nm_v, ng_v, mg_v, m1o_v, m2o_v, keys_v,
     send_sem, recv_sem, local_sem, met,
 ):
     rep = lax.axis_index("rep")
@@ -201,12 +201,19 @@
         def _():
             signal(met.at[MET_ZL], chip_zl(peer))
 
-    wz = remote("wz", 0, 0, w_o.at[own_rows], w_p.at[own_rows], partner)
+    def half_rows(half):
+        return pl.ds(pl.multiple_of(core * ROWS + half * (ROWS // 2), ROWS // 2), ROWS // 2)
+
+    wz = [
+        remote("wz", half, half, w_o.at[half_rows(half)], w_p.at[half_rows(half)], partner)
+        for half in range(2)
+    ]
     wsib = remote("wsib", 0, 0, w_o.at[own_rows], w_o.at[own_rows], sibling)
 
     @pl.when(zh == 1)
     def _():
-        wz.start()
+        wz[0].start()
+        wz[1].start()
 
     @pl.when(core == 1)
     def _():
@@ -275,7 +282,8 @@
     @pl.when(zh == 0)
     def _():
         pl.semaphore_wait(met.at[MET_Z], 1)
-        wz.start()
+        wz[0].start()
+        wz[1].start()
 
     wsib.wait_recv()
     wait_x("u", tall)
@@ -294,19 +302,18 @@
     total = dr_v[:, y].reshape(N_ZL * 8, COLS)
     for e in range(N_Y - 1):
         total = total + dr_all[e].astype(F32)
-    ds[...] = total
-    ds_low[...] = total.astype(BF16)
+    ds[...] = total.reshape(N_ZL, 8, COLS)
     loads["mo"].wait()
     loads["gl"].wait()
-    base[zl] = gl_v[...] - (outer_rate * outer_beta * outer_beta) * mo_v[...]
+    with_base[...] = ds[...]
+    base = gl_v[...] - (outer_rate * outer_beta * outer_beta) * mo_v[...]
+    with_base[zl] = ds[zl] - (N_REP / (outer_rate * (1.0 + outer_beta))) * base
+    ds_low[...] = with_base[...].reshape(N_ZL * 8, COLS).astype(BF16)
     dz_copy = [
         remote("dz", f - 1, f - 1, ds_low, dz.at[f - 1], at_zl(f)) for f in range(1, N_ZL)
     ]
-    base_copy = [
-        remote("base", f - 1, f - 1, base.at[zl], base.at[zl], at_zl(f)) for f in range(1, N_ZL)
-    ]
     wait_for(met.at[MET_ZL], N_ZL - 1 - zl)
-    for copy in dz_copy + base_copy:
+    for copy in dz_copy:
         copy.start()
 
     loads["ap"].wait()
@@ -318,12 +325,23 @@
     gpsib = remote("gpsib", 0, 0, gp_send, gp_recv, sibling)
     gpsib.start()
 
-    wz.wait_recv()
-    wfwd = remote("wfwd", 0, 0, w_p.at[own_rows], w_p.at[own_rows], sibling)
-    wfwd.start()
     gpsib.wait_recv()
     gz_send[...] = (gp[own_rows, :] + gp_recv[...].astype(F32)).astype(BF16)
-    wfwd.wait_recv()
+    gz = remote("gz", 0, 0, gz_send, gz_recv, partner)
+
+    @pl.when(zh == 1)
+    def _():
+        gz.start()
+
+    wfwd = [
+        remote("wfwd", half, half, w_p.at[half_rows(half)], w_p.at[half_rows(half)], sibling)
+        for half in range(2)
+    ]
+    for half in range(2):
+        wz[half].wait_recv()
+        wfwd[half].start()
+    for copy in wfwd:
+        copy.wait_recv()
 
     ig_p[...] = lax.dot_general(
         u_all[...], w_p[...], (((1,), (1,)), ((), ())), preferred_element_type=F32
@@ -335,19 +353,49 @@
     outs.append(local("igp", ig_p.at[slot(x)], ig_out.at[0, :, columns(1 - zh, x)]))
     outs[-1].start()
 
-    for copy in dz_copy + base_copy:
+    loads["ao"].wait()
+    wait_x("ao", tall)
+    go[...] = lax.dot_general(
+        ao[...], u_all[...], (((0,), (0,)), ((), ())), preferred_element_type=F32
+    )
+    go_send[...] = go[sib_rows, :].astype(BF16)
+    gosib = remote("gosib", 0, 0, go_send, go_recv, sibling)
+    gosib.start()
+
+    pk_copy = to_x("pk", lambda peer: pk_send.at[peer], lambda peer: pk_recv.at[(peer - x + 3) % 4])
+    for peer in range(N_X):
+        part = jnp.dot(ao[slot(peer), :], w_o[...], preferred_element_type=F32)
+        part += jnp.dot(ap[slot(peer), :], w_p[...], preferred_element_type=F32)
+
+        @pl.when(peer == x)
+        def _():
+            pk_own[...] = part
+
+        @pl.when(peer != x)
+        def _():
+            pk_send[peer] = part.astype(BF16)
+            pk_copy[peer].start()
+
+    @pl.when(zh == 0)
+    def _():
+        gz.start()
+
+    for copy in dz_copy:
         copy.wait_recv()
-    total = ds[...]
+    total = with_base[...].reshape(N_ZL * 8, COLS)
     for step in range(N_ZL - 1):
         total = total + dz[step].astype(F32)
-    mean_all[...] = (total / N_REP).reshape(N_ZL, 8, COLS)
-    fresh = base[...] - (outer_rate * (1.0 + outer_beta)) * mean_all[...]
-    ga_low[...] = fresh.reshape(N_ZL * 8, COLS).astype(BF16)
+    ga_low[...] = ((-outer_rate * (1.0 + outer_beta) / N_REP) * total).astype(BF16)
     ay_copy = [remote("ay", e - 1, e - 1, ga_low, gg.at[y], at_y(e)) for e in range(1, N_Y)]
     for copy in ay_copy:
         copy.start()
     gg[y] = ga_low[...]
-    mean_drift = mean_all[zl]
+    own_piece = pl.ds(pl.multiple_of(zl * 8, 8), 8)
+    own_total = ds[zl]
+    for step in range(N_ZL - 1):
+        dz_wide[step] = dz[step].astype(F32)
+        own_total = own_total + dz_wide[step, own_piece, :]
+    mean_drift = own_total / N_REP
     moment = outer_beta * mo_v[...] + mean_drift
     nm_v[...] = moment
     ng_v[...] = gl_v[...] - outer_rate * (mean_drift + outer_beta * moment)
@@ -355,32 +403,6 @@
     outs[-1].start()
     outs.append(local("ng", ng_v, ng_out))
     outs[-1].start()
-
-    gz = remote("gz", 0, 0, gz_send, gz_recv, partner)
-    gz.start()
-
-    loads["ao"].wait()
-    wait_x("ao", tall)
-    go[...] = lax.dot_general(
-        ao[...], u_all[...], (((0,), (0,)), ((), ())), preferred_element_type=F32
-    )
-    go_send[...] = go[sib_rows, :].astype(BF16)
-    gosib = remote("gosib", 0, 0, go_send, go_recv, sibling)
-    gosib.start()
-
-    pk_copy = to_x("pk", lambda peer: pk_send.at[peer], lambda peer: pk_recv.at[(peer - x + 3) % 4])
-    for peer in range(N_X):
-        part = jnp.dot(ao[slot(peer), :], w_o[...], preferred_element_type=F32)
-        part += jnp.dot(ap[slot(peer), :], w_p[...], preferred_element_type=F32)
-
-        @pl.when(peer == x)
-        def _():
-            pk_own[...] = part
-
-        @pl.when(peer != x)
-        def _():
-            pk_send[peer] = part.astype(BF16)
-            pk_copy[peer].start()
 
     loads["m1"].wait()
     loads["m2"].wait()
@@ -424,32 +446,21 @@
     wait_x("igp", tall)
     for copies in (u_copy, ap_copy, ao_copy, igo_copy, igp_copy, pk_copy):
         each_peer(lambda peer: copies[peer].wait_send())
-    for copy in dy_copy + dz_copy + base_copy + ay_copy + [wz, wsib, wfwd, gpsib, gosib, gz]:
+    for copy in dy_copy + dz_copy + ay_copy + wz + wfwd + [wsib, gpsib, gosib, gz]:
         copy.wait_send()
     for copy in outs:
         copy.wait()
 
 
-PIECES = ((1, 32), (1, 32), (1, 32), (1, 32), (2, 128), (2, 128), (3, 256), (4, 256), (0, 128), (5, 8), (6, 8))
-
-
 def hand_over(*refs):
-    given, taken, held, sems = refs[:7], refs[7:14], refs[14:21], refs[21]
-    loads, stores, done = [], [], [0] * 7
-    for at, (which, rows) in enumerate(PIECES):
-        src, dst = given[which], taken[which]
-        if which < 5:
-            src, dst = src.at[0], dst.at[0]
-        part = pl.ds(done[which], rows)
-        done[which] += rows
-        loads.append(pltpu.make_async_copy(src.at[part], held[which].at[part], sems.at[0, at]))
-        stores.append(pltpu.make_async_copy(held[which].at[part], dst.at[part], sems.at[1, at]))
-    for copy in loads:
+    given, taken, sems = refs[:7], refs[7:14], refs[14]
+    copies = [
+        pltpu.make_async_copy(src, dst, sems.at[at])
+        for at, (src, dst) in enumerate(zip(given, taken))
+    ]
+    for copy in copies:
         copy.start()
-    for load, store in zip(loads, stores):
-        load.wait()
-        store.start()
-    for copy in stores:
+    for copy in copies:
         copy.wait()
 
 
@@ -468,8 +479,8 @@
         vmem((ROWS, COLS), BF16), vmem((ROWS, COLS), BF16), vmem((ROWS, COLS), BF16),
         vmem((ROWS, COLS), BF16), vmem((ROWS, COLS), BF16), vmem((ROWS, COLS), BF16),
         vmem((N_ZL, N_Y, 8, COLS), F32), vmem((N_Y, N_ZL * 8, COLS), BF16), vmem((N_Y - 1, N_ZL * 8, COLS), BF16),
-        vmem((N_ZL * 8, COLS), F32), vmem((N_ZL * 8, COLS), BF16),
-        vmem((3, N_ZL * 8, COLS), BF16), vmem(piece, F32), vmem(piece, F32), vmem((N_ZL * 8, COLS), BF16),
+        vmem(piece, F32), vmem(piece, F32), vmem((N_ZL * 8, COLS), BF16),
+        vmem((3, N_ZL * 8, COLS), BF16), vmem((3, N_ZL * 8, COLS), F32), vmem((N_ZL * 8, COLS), BF16),
         vmem((N_Y, N_ZL * 8, COLS), BF16), vmem((8, COLS), F32), vmem((8, COLS), F32), vmem((ROWS, COLS), F32),
         vmem((ROWS, COLS), BF16), vmem((ROWS, COLS), BF16), vmem((TOK, COLS), BF16),
         pltpu.SemaphoreType.DMA((N_REMOTE,)), pltpu.SemaphoreType.DMA((N_REMOTE,)),
@@ -483,7 +494,7 @@
     anywhere = pl.BlockSpec(memory_space=pl.ANY)
     results = pl.pallas_call(
         kernel,
-        out_shape=outs,
+        out_shape=tuple(vmem(out.shape, out.dtype) for out in outs),
         in_specs=[anywhere] * 9,
         out_specs=[anywhere] * 7,
         scratch_shapes=scratch,
@@ -499,10 +510,9 @@
         out_shape=outs,
         in_specs=[anywhere] * 7,
         out_specs=[anywhere] * 7,
-        scratch_shapes=[vmem(out.shape[-2:], out.dtype) for out in outs]
-        + [pltpu.SemaphoreType.DMA((2, len(PIECES)))],
+        scratch_shapes=[pltpu.SemaphoreType.DMA((7,))],
         compiler_params=pltpu.CompilerParams(vmem_limit_bytes=56 * 2**20),
-    )(*results)
+    )(*[pltpu.with_memory_space_constraint(result, pltpu.VMEM) for result in results])
 
 
 def solution(mesh):

time: 50.5 us -> 48.8 us (0.966)
  the two profiles are of different devices: /device:TPU:70 before, /device:TPU:63 now
where the time goes in v3:
time: 48.8 us; the launch traced here: 48.7 us
  Pallas kernels  48.1 us (99%)
  between operations  0.64 us (1%)
    pallas_call x1, Pallas kernels, body(): pl.pallas_call(kernel, out_shape=tuple((vmem(out.shape, out.dtype) for ou...  46.6 us
    pallas_call x1, Pallas kernels, body(): pl.pallas_call(hand_over, out_shape=outs, in_specs=[anywhere] * 7, out_sp...  1.42 us

profile of v3, /device:TPU:63, one launch (start us, length us, event | category | flops | bytes accessed | tf_op | source)
XLA Modules:
  0.0 48.7 jit_solution(14139554861331209172)
XLA Ops:
  0.6 46.6 %shard_map.144 = (bf16[1,128,512]{2,1,0:T(8,128)(2,1)S(1)}, bf16[1,128,4096]{2,1,0:T(8,128)(2,1)S(1)}, f32[1,256,512]{2,1,0:T(8,128)S(1)}, bf16[1,256,512]{2,1,0...) custom-call(bf16[1,128,4096]{2,1,0:T(8,128)(2,1)} %inp.1, ...), custom_call_target="tpu_custom_call" | custom-call | tf_op jit(solution)/shard_map/pallas_call | solution.py:495
  47.3 1.4 %shard_map.145 = (bf16[1,128,512]{2,1,0:T(8,128)(2,1)}, bf16[1,128,4096]{2,1,0:T(8,128)(2,1)}, f32[1,256,512]{2,1,0:T(8,128)}, bf16[1,256,512]{2,1,0:T(8,128)(2,...) custom-call(bf16[1,128,512]{2,1,0:T(8,128)(2,1)S(1)} %get-tuple-element.14.refs_0_, ...), custom_call_target="tpu_custom_call" | custom-call | tf_op jit(solution)/shard_map/pallas_call | solution.py:508

commit v4 on v3

--- a/solution.py
+++ b/solution.py
@@ -69,7 +69,8 @@
 for _name, _count in REMOTE:
     FIRST[_name] = N_REMOTE
     N_REMOTE += _count
-MET_SIB, MET_Z, MET_Y, MET_ZL = N_X, N_X + 1, N_X + 2, N_X + 3
+MET_Z, MET_Y, MET_ZL = 0, 1, 2
+FAR_FIRST = (4, 3, 5, 2, 6, 1, 7)
 
 
 def kernel(
@@ -131,10 +132,9 @@
         return pl.ds(pl.multiple_of(chip * TOK, TOK), TOK)
 
     barrier = pltpu.get_barrier_semaphore()
-    for peer in range(1, N_X):
-        @pl.when(peer > x)
-        def _():
-            signal(barrier, chip_x(peer))
+    for step in range(1, N_X):
+        signal(barrier, chip_x((x + step) % N_X))
+    signal(barrier, sibling)
     for peer in range(1, N_Y):
         @pl.when(peer > y)
         def _():
@@ -143,10 +143,6 @@
         @pl.when(peer > zl)
         def _():
             signal(barrier, chip_zl(peer))
-
-    @pl.when(core == 0)
-    def _():
-        signal(barrier, sibling)
 
     @pl.when(zh == 0)
     def _():
@@ -164,8 +160,26 @@
         "mo": local("mo", mo, mo_v),
         "gl": local("gl", gl, gl_v),
     }
-    for copy in loads.values():
-        copy.start()
+    for name in ("kg", "tab", "w", "dr"):
+        loads[name].start()
+
+    pl.semaphore_wait(barrier, N_X + y + zl + zh)
+
+    @pl.when(zh == 1)
+    def _():
+        signal(met.at[MET_Z], partner)
+
+    for peer in range(N_Y - 1):
+        @pl.when(peer < y)
+        def _():
+            signal(met.at[MET_Y], chip_y(peer))
+    for peer in range(N_ZL - 1):
+        @pl.when(peer < zl)
+        def _():
+            signal(met.at[MET_ZL], chip_zl(peer))
+
+    for name in ("ap", "ao", "m1", "m2", "mo", "gl"):
+        loads[name].start()
 
     loads["kg"].wait()
     loads["tab"].wait()
@@ -178,28 +192,8 @@
     for peer in range(N_Y):
         dr_low[peer] = dr_v[:, peer].reshape(N_ZL * 8, COLS).astype(BF16)
 
-    wait_for(barrier, x + y + zl + core + zh)
-    for peer in range(N_X - 1):
-        @pl.when(peer < x)
-        def _():
-            signal(met.at[x], chip_x(peer))
-
-    @pl.when(core == 1)
-    def _():
-        signal(met.at[MET_SIB], sibling)
-
-    @pl.when(zh == 1)
-    def _():
-        signal(met.at[MET_Z], partner)
-
-    for peer in range(N_Y - 1):
-        @pl.when(peer < y)
-        def _():
-            signal(met.at[MET_Y], chip_y(peer))
-    for peer in range(N_ZL - 1):
-        @pl.when(peer < zl)
-        def _():
-            signal(met.at[MET_ZL], chip_zl(peer))
+    ahead = zl < N_ZL // 2
+    behind = jnp.logical_not(ahead)
 
     def half_rows(half):
         return pl.ds(pl.multiple_of(core * ROWS + half * (ROWS // 2), ROWS // 2), ROWS // 2)
@@ -215,9 +209,7 @@
         wz[0].start()
         wz[1].start()
 
-    @pl.when(core == 1)
-    def _():
-        wsib.start()
+    wsib.start()
 
     def to_x(name, src, dst):
         return [remote(name, peer, x, src(peer), dst(peer), chip_x(peer)) for peer in range(N_X)]
@@ -241,41 +233,16 @@
         "ao", lambda peer: inp.at[0, :, columns(zh, peer)], lambda peer: ao.at[slot(x)]
     )
 
-    def first_sends(peer):
-        @pl.when(peer > x)
-        def _():
-            pl.semaphore_wait(met.at[peer], 1)
-
-        u_copy[peer].start()
-
-    late = (zh == 1) & (core == 1)
-    for peer in range(N_X - 1):
-        pl.when(peer != x)(functools.partial(first_sends, peer))
-
-    @pl.when((x != N_X - 1) & jnp.logical_not(late))
-    def _():
-        first_sends(N_X - 1)
-
-    for peer in range(N_X):
-        pl.when((peer != x) & ((peer < N_X - 1) | jnp.logical_not(late)))(ap_copy[peer].start)
+    each_peer(lambda peer: u_copy[peer].start())
+    each_peer(lambda peer: ap_copy[peer].start())
 
     dy_copy = [
         remote("dy", e - 1, e - 1, dr_low.at[(y + e) % N_Y], dr_all.at[e - 1], at_y(e))
         for e in range(1, N_Y)
     ]
     wait_for(met.at[MET_Y], N_Y - 1 - y)
-    for copy in dy_copy:
-        copy.start()
-
-    @pl.when((x != N_X - 1) & late)
-    def _():
-        first_sends(N_X - 1)
-        ap_copy[N_X - 1].start()
-
-    @pl.when(core == 0)
-    def _():
-        pl.semaphore_wait(met.at[MET_SIB], 1)
-        wsib.start()
+    for e in FAR_FIRST:
+        dy_copy[e - 1].start()
 
     each_peer(lambda peer: ao_copy[peer].start())
 
@@ -387,8 +354,8 @@
         total = total + dz[step].astype(F32)
     ga_low[...] = ((-outer_rate * (1.0 + outer_beta) / N_REP) * total).astype(BF16)
     ay_copy = [remote("ay", e - 1, e - 1, ga_low, gg.at[y], at_y(e)) for e in range(1, N_Y)]
-    for copy in ay_copy:
-        copy.start()
+    for e in FAR_FIRST:
+        ay_copy[e - 1].start()
     gg[y] = ga_low[...]
     own_piece = pl.ds(pl.multiple_of(zl * 8, 8), 8)
     own_total = ds[zl]
@@ -484,7 +451,7 @@
         vmem((N_Y, N_ZL * 8, COLS), BF16), vmem((8, COLS), F32), vmem((8, COLS), F32), vmem((ROWS, COLS), F32),
         vmem((ROWS, COLS), BF16), vmem((ROWS, COLS), BF16), vmem((TOK, COLS), BF16),
         pltpu.SemaphoreType.DMA((N_REMOTE,)), pltpu.SemaphoreType.DMA((N_REMOTE,)),
-        pltpu.SemaphoreType.DMA((len(LOCAL),)), pltpu.SemaphoreType.REGULAR((N_X + 4,)),
+        pltpu.SemaphoreType.DMA((len(LOCAL),)), pltpu.SemaphoreType.REGULAR((3,)),
     ]
     outs = (
         shape((1, TOK, COLS), BF16), shape((1, TOK, WIN), BF16), shape((1, ROWS, COLS), F32),

time: 48.8 us -> 45.6 us (0.934)
  the two profiles are of different devices: /device:TPU:63 before, /device:TPU:4 now
where the time goes in v4:
time: 45.6 us; the launch traced here: 45.5 us
  Pallas kernels  44.8 us (98%)
  between operations  0.64 us (1%)
    pallas_call x1, Pallas kernels, body(): pl.pallas_call(kernel, out_shape=tuple((vmem(out.shape, out.dtype) for ou...  43.4 us
    pallas_call x1, Pallas kernels, body(): pl.pallas_call(hand_over, out_shape=outs, in_specs=[anywhere] * 7, out_sp...  1.42 us

profile of v4, /device:TPU:4, one launch (start us, length us, event | category | flops | bytes accessed | tf_op | source)
XLA Modules:
  0.0 45.5 jit_solution(2928748778648130960)
XLA Ops:
  0.6 43.4 %shard_map.144 = (bf16[1,128,512]{2,1,0:T(8,128)(2,1)S(1)}, bf16[1,128,4096]{2,1,0:T(8,128)(2,1)S(1)}, f32[1,256,512]{2,1,0:T(8,128)S(1)}, bf16[1,256,512]{2,1,0...) custom-call(bf16[1,128,4096]{2,1,0:T(8,128)(2,1)} %inp.1, ...), custom_call_target="tpu_custom_call" | custom-call | tf_op jit(solution)/shard_map/pallas_call | solution.py:462
  44.1 1.4 %shard_map.145 = (bf16[1,128,512]{2,1,0:T(8,128)(2,1)}, bf16[1,128,4096]{2,1,0:T(8,128)(2,1)}, f32[1,256,512]{2,1,0:T(8,128)}, bf16[1,256,512]{2,1,0:T(8,128)(2,...) custom-call(bf16[1,128,512]{2,1,0:T(8,128)(2,1)S(1)} %get-tuple-element.14.refs_0_, ...), custom_call_target="tpu_custom_call" | custom-call | tf_op jit(solution)/shard_map/pallas_call | solution.py:475

commit v5 on v4

--- a/solution.py
+++ b/solution.py
@@ -55,20 +55,18 @@
     return jnp.concatenate(heads, axis=1)
 
 
-REMOTE = (
-    ("u", N_X), ("ap", N_X), ("ao", N_X), ("igo", N_X), ("igp", N_X), ("pk", N_X),
-    ("wsib", 1), ("wz", 2), ("wfwd", 2), ("gpsib", 1), ("gosib", 1), ("gz", 1),
-    ("dy", 7), ("dz", 3), ("ay", 7),
-)
-LOCAL = (
-    "kg", "tab", "w", "m1", "m2", "mo", "gl", "ap", "ao", "dr",
-    "igo", "igp", "mg", "m1o", "m2o", "nm", "ng", "keys",
-)
-FIRST = {}
-N_REMOTE = 0
-for _name, _count in REMOTE:
-    FIRST[_name] = N_REMOTE
-    N_REMOTE += _count
+SEND = {}
+for _at, _names in enumerate((
+    ("u",), ("ap",), ("ao",), ("igo",), ("igp",), ("pk",), ("wsib", "wz", "wfwd", "gpsib"),
+    ("gosib", "gz"), ("dz",), ("dy",), ("ay",),
+)):
+    SEND.update({_name: _at for _name in _names})
+RECV = {"u": 0, "ap": 1, "ao": 2, "igo": 3, "igp": 4, "pk": 5, "wsib": 6, "wz": 7, "wfwd": 9,
+        "gpsib": 10, "gosib": 11, "gz": 12, "dz": 13, "dy": 14, "ay": 15}
+N_SEND, N_RECV = 11, 16
+LOCAL = {"kg": 0, "tab": 1, "w": 2, "dr": 3, "ap": 4, "ao": 5, "m1": 6, "m2": 6, "mo": 7, "gl": 8,
+         "igo": 9, "igp": 9, "mg": 10, "m1o": 10, "m2o": 10, "nm": 11, "ng": 12, "keys": 13}
+N_LOCAL = 14
 MET_Z, MET_Y, MET_ZL = 0, 1, 2
 FAR_FIRST = (4, 3, 5, 2, 6, 1, 7)
 
@@ -105,14 +103,20 @@
     sibling = (rep, zh * 8 + x * 2 + (1 - core))
     partner = (rep, (1 - zh) * 8 + x * 2 + core)
 
-    def remote(name, send, recv, src, dst, device):
+    def remote(name, src, dst, device, part=0):
         return pltpu.make_async_remote_copy(
-            src_ref=src, dst_ref=dst, send_sem=send_sem.at[FIRST[name] + send],
-            recv_sem=recv_sem.at[FIRST[name] + recv], device_id=device, device_id_type=MESH,
+            src_ref=src, dst_ref=dst, send_sem=send_sem.at[SEND[name]],
+            recv_sem=recv_sem.at[RECV[name] + part], device_id=device, device_id_type=MESH,
         )
 
     def local(name, src, dst):
-        return pltpu.make_async_copy(src, dst, local_sem.at[LOCAL.index(name)])
+        return pltpu.make_async_copy(src, dst, local_sem.at[LOCAL[name]])
+
+    def arrived(name, size_of):
+        remote(name, size_of, size_of, sibling).wait_recv()
+
+    def sent(name, size_of):
+        remote(name, size_of, size_of, sibling).wait_send()
 
     def signal(semaphore, device):
         pl.semaphore_signal(semaphore, inc=1, device_id=device, device_id_type=MESH)
@@ -199,10 +203,10 @@
         return pl.ds(pl.multiple_of(core * ROWS + half * (ROWS // 2), ROWS // 2), ROWS // 2)
 
     wz = [
-        remote("wz", half, half, w_o.at[half_rows(half)], w_p.at[half_rows(half)], partner)
+        remote("wz", w_o.at[half_rows(half)], w_p.at[half_rows(half)], partner, half)
         for half in range(2)
     ]
-    wsib = remote("wsib", 0, 0, w_o.at[own_rows], w_o.at[own_rows], sibling)
+    wsib = remote("wsib", w_o.at[own_rows], w_o.at[own_rows], sibling)
 
     @pl.when(zh == 1)
     def _():
@@ -212,19 +216,12 @@
     wsib.start()
 
     def to_x(name, src, dst):
-        return [remote(name, peer, x, src(peer), dst(peer), chip_x(peer)) for peer in range(N_X)]
+        return [remote(name, src(peer), dst(peer), chip_x(peer)) for peer in range(N_X)]
 
     def each_peer(act):
         for peer in range(N_X):
             pl.when(peer != x)(functools.partial(act, peer))
 
-    def wait_x(name, shape_of):
-        def wait(peer):
-            remote(name, peer, peer, shape_of, shape_of, chip_x(peer)).wait_recv()
-
-        each_peer(wait)
-
-    tall = u_all.at[slot(0)]
     u_copy = to_x("u", lambda peer: u_all.at[slot(x)], lambda peer: u_all.at[slot(x)])
     ap_copy = to_x(
         "ap", lambda peer: inp.at[0, :, columns(1 - zh, peer)], lambda peer: ap.at[slot(x)]
@@ -237,7 +234,7 @@
     each_peer(lambda peer: ap_copy[peer].start())
 
     dy_copy = [
-        remote("dy", e - 1, e - 1, dr_low.at[(y + e) % N_Y], dr_all.at[e - 1], at_y(e))
+        remote("dy", dr_low.at[(y + e) % N_Y], dr_all.at[e - 1], at_y(e))
         for e in range(1, N_Y)
     ]
     wait_for(met.at[MET_Y], N_Y - 1 - y)
@@ -253,7 +250,7 @@
         wz[1].start()
 
     wsib.wait_recv()
-    wait_x("u", tall)
+    arrived("u", pk_recv)
     ig_o[...] = lax.dot_general(
         u_all[...], w_o[...], (((1,), (1,)), ((), ())), preferred_element_type=F32
     ).astype(BF16)
@@ -261,11 +258,9 @@
         "igo", lambda peer: ig_o.at[slot(peer)], lambda peer: ig_out.at[0, :, columns(zh, x)]
     )
     each_peer(lambda peer: igo_copy[peer].start())
-    outs = [local("igo", ig_o.at[slot(x)], ig_out.at[0, :, columns(zh, x)])]
-    outs[0].start()
-
-    for copy in dy_copy:
-        copy.wait_recv()
+    local("igo", ig_o.at[slot(x)], ig_out.at[0, :, columns(zh, x)]).start()
+
+    arrived("dy", dr_all)
     total = dr_v[:, y].reshape(N_ZL * 8, COLS)
     for e in range(N_Y - 1):
         total = total + dr_all[e].astype(F32)
@@ -277,38 +272,37 @@
     with_base[zl] = ds[zl] - (N_REP / (outer_rate * (1.0 + outer_beta))) * base
     ds_low[...] = with_base[...].reshape(N_ZL * 8, COLS).astype(BF16)
     dz_copy = [
-        remote("dz", f - 1, f - 1, ds_low, dz.at[f - 1], at_zl(f)) for f in range(1, N_ZL)
+        remote("dz", ds_low, dz.at[f - 1], at_zl(f)) for f in range(1, N_ZL)
     ]
     wait_for(met.at[MET_ZL], N_ZL - 1 - zl)
     for copy in dz_copy:
         copy.start()
 
     loads["ap"].wait()
-    wait_x("ap", tall)
+    arrived("ap", pk_recv)
     gp[...] = lax.dot_general(
         ap[...], u_all[...], (((0,), (0,)), ((), ())), preferred_element_type=F32
     )
     gp_send[...] = gp[sib_rows, :].astype(BF16)
-    gpsib = remote("gpsib", 0, 0, gp_send, gp_recv, sibling)
+    gpsib = remote("gpsib", gp_send, gp_recv, sibling)
     gpsib.start()
 
     gpsib.wait_recv()
     gz_send[...] = (gp[own_rows, :] + gp_recv[...].astype(F32)).astype(BF16)
-    gz = remote("gz", 0, 0, gz_send, gz_recv, partner)
+    gz = remote("gz", gz_send, gz_recv, partner)
 
     @pl.when(zh == 1)
     def _():
         gz.start()
 
     wfwd = [
-        remote("wfwd", half, half, w_p.at[half_rows(half)], w_p.at[half_rows(half)], sibling)
+        remote("wfwd", w_p.at[half_rows(half)], w_p.at[half_rows(half)], sibling)
         for half in range(2)
     ]
     for half in range(2):
         wz[half].wait_recv()
         wfwd[half].start()
-    for copy in wfwd:
-        copy.wait_recv()
+    arrived("wfwd", gz_send)
 
     ig_p[...] = lax.dot_general(
         u_all[...], w_p[...], (((1,), (1,)), ((), ())), preferred_element_type=F32
@@ -317,16 +311,15 @@
         "igp", lambda peer: ig_p.at[slot(peer)], lambda peer: ig_out.at[0, :, columns(1 - zh, x)]
     )
     each_peer(lambda peer: igp_copy[peer].start())
-    outs.append(local("igp", ig_p.at[slot(x)], ig_out.at[0, :, columns(1 - zh, x)]))
-    outs[-1].start()
+    local("igp", ig_p.at[slot(x)], ig_out.at[0, :, columns(1 - zh, x)]).start()
 
     loads["ao"].wait()
-    wait_x("ao", tall)
+    arrived("ao", pk_recv)
     go[...] = lax.dot_general(
         ao[...], u_all[...], (((0,), (0,)), ((), ())), preferred_element_type=F32
     )
     go_send[...] = go[sib_rows, :].astype(BF16)
-    gosib = remote("gosib", 0, 0, go_send, go_recv, sibling)
+    gosib = remote("gosib", go_send, go_recv, sibling)
     gosib.start()
 
     pk_copy = to_x("pk", lambda peer: pk_send.at[peer], lambda peer: pk_recv.at[(peer - x + 3) % 4])
@@ -347,13 +340,12 @@
     def _():
         gz.start()
 
-    for copy in dz_copy:
-        copy.wait_recv()
+    arrived("dz", dz)
     total = with_base[...].reshape(N_ZL * 8, COLS)
     for step in range(N_ZL - 1):
         total = total + dz[step].astype(F32)
     ga_low[...] = ((-outer_rate * (1.0 + outer_beta) / N_REP) * total).astype(BF16)
-    ay_copy = [remote("ay", e - 1, e - 1, ga_low, gg.at[y], at_y(e)) for e in range(1, N_Y)]
+    ay_copy = [remote("ay", ga_low, gg.at[y], at_y(e)) for e in range(1, N_Y)]
     for e in FAR_FIRST:
         ay_copy[e - 1].start()
     gg[y] = ga_low[...]
@@ -366,16 +358,14 @@
     moment = outer_beta * mo_v[...] + mean_drift
     nm_v[...] = moment
     ng_v[...] = gl_v[...] - outer_rate * (mean_drift + outer_beta * moment)
-    outs.append(local("nm", nm_v, nm_out))
+    outs = [local("nm", nm_v, nm_out)]
     outs[-1].start()
     outs.append(local("ng", ng_v, ng_out))
     outs[-1].start()
 
-    loads["m1"].wait()
-    loads["m2"].wait()
+    local("m1", u_all, u_all).wait()
     gosib.wait_recv()
-    for copy in ay_copy:
-        copy.wait_recv()
+    arrived("ay", dr_all)
     gz.wait_recv()
 
     for zone in range(N_ZL):
@@ -398,10 +388,9 @@
         m1o_v[rows, :] = moment_one.astype(BF16)
         m2o_v[rows, :] = moment_two.astype(BF16)
     for name, src, dst in (("mg", mg_v, mg_out), ("m1o", m1o_v, m1_out), ("m2o", m2o_v, m2_out)):
-        outs.append(local(name, src, dst.at[0]))
-        outs[-1].start()
-
-    wait_x("pk", tall)
+        local(name, src, dst.at[0]).start()
+
+    arrived("pk", pk_recv)
     projected = pk_own[...]
     for step in range(3):
         projected = projected + pk_recv[step].astype(F32)
@@ -409,12 +398,17 @@
     outs.append(local("keys", keys_v, keys_out.at[0]))
     outs[-1].start()
 
-    wait_x("igo", tall)
-    wait_x("igp", tall)
-    for copies in (u_copy, ap_copy, ao_copy, igo_copy, igp_copy, pk_copy):
-        each_peer(lambda peer: copies[peer].wait_send())
-    for copy in dy_copy + dz_copy + ay_copy + wz + wfwd + [wsib, gpsib, gosib, gz]:
-        copy.wait_send()
+    arrived("igo", pk_recv)
+    arrived("igp", pk_recv)
+    for name in ("u", "ap", "ao", "igo", "igp", "pk"):
+        sent(name, pk_recv)
+    sent("wsib", gp)
+    sent("gosib", u_all)
+    sent("dz", dz)
+    sent("dy", dr_all)
+    sent("ay", dr_all)
+    local("igo", gz_send, gz_send).wait()
+    local("mg", gp, gp).wait()
     for copy in outs:
         copy.wait()
 
@@ -450,8 +444,8 @@
         vmem((3, N_ZL * 8, COLS), BF16), vmem((3, N_ZL * 8, COLS), F32), vmem((N_ZL * 8, COLS), BF16),
         vmem((N_Y, N_ZL * 8, COLS), BF16), vmem((8, COLS), F32), vmem((8, COLS), F32), vmem((ROWS, COLS), F32),
         vmem((ROWS, COLS), BF16), vmem((ROWS, COLS), BF16), vmem((TOK, COLS), BF16),
-        pltpu.SemaphoreType.DMA((N_REMOTE,)), pltpu.SemaphoreType.DMA((N_REMOTE,)),
-        pltpu.SemaphoreType.DMA((len(LOCAL),)), pltpu.SemaphoreType.REGULAR((3,)),
+        pltpu.SemaphoreType.DMA((N_SEND,)), pltpu.SemaphoreType.DMA((N_RECV,)),
+        pltpu.SemaphoreType.DMA((N_LOCAL,)), pltpu.SemaphoreType.REGULAR((3,)),
     ]
     outs = (
         shape((1, TOK, COLS), BF16), shape((1, TOK, WIN), BF16), shape((1, ROWS, COLS), F32),

time: 45.6 us -> 44.9 us (0.985)
  Pallas kernels: 44.8 us -> 44.1 us
    pallas_call x1, Pallas kernels: 43.4 us -> 42.7 us  [body(): pl.pallas_call(kernel, out_shape=tuple((vmem(out.shape, out.dtype) for ou...]
where the time goes in v5:
time: 44.9 us; the launch traced here: 44.7 us
  Pallas kernels  44.1 us (98%)
  between operations  0.64 us (1%)
    pallas_call x1, Pallas kernels, body(): pl.pallas_call(kernel, out_shape=tuple((vmem(out.shape, out.dtype) for ou...  42.7 us
    pallas_call x1, Pallas kernels, body(): pl.pallas_call(hand_over, out_shape=outs, in_specs=[anywhere] * 7, out_sp...  1.42 us

profile of v5, /device:TPU:4, one launch (start us, length us, event | category | flops | bytes accessed | tf_op | source)
XLA Modules:
  0.0 44.7 jit_solution(16926660952646394202)
XLA Ops:
  0.6 42.7 %shard_map.144 = (bf16[1,128,512]{2,1,0:T(8,128)(2,1)S(1)}, bf16[1,128,4096]{2,1,0:T(8,128)(2,1)S(1)}, f32[1,256,512]{2,1,0:T(8,128)S(1)}, bf16[1,256,512]{2,1,0...) custom-call(bf16[1,128,4096]{2,1,0:T(8,128)(2,1)} %inp.1, ...), custom_call_target="tpu_custom_call" | custom-call | tf_op jit(solution)/shard_map/pallas_call | solution.py:456
  43.3 1.4 %shard_map.145 = (bf16[1,128,512]{2,1,0:T(8,128)(2,1)}, bf16[1,128,4096]{2,1,0:T(8,128)(2,1)}, f32[1,256,512]{2,1,0:T(8,128)}, bf16[1,256,512]{2,1,0:T(8,128)(2,...) custom-call(bf16[1,128,512]{2,1,0:T(8,128)(2,1)S(1)} %get-tuple-element.14.refs_0_, ...), custom_call_target="tpu_custom_call" | custom-call | tf_op jit(solution)/shard_map/pallas_call | solution.py:469

commit v6 on v5

--- a/solution.py
+++ b/solution.py
@@ -65,8 +65,8 @@
         "gpsib": 10, "gosib": 11, "gz": 12, "dz": 13, "dy": 14, "ay": 15}
 N_SEND, N_RECV = 11, 16
 LOCAL = {"kg": 0, "tab": 1, "w": 2, "dr": 3, "ap": 4, "ao": 5, "m1": 6, "m2": 6, "mo": 7, "gl": 8,
-         "igo": 9, "igp": 9, "mg": 10, "m1o": 10, "m2o": 10, "nm": 11, "ng": 12, "keys": 13}
-N_LOCAL = 14
+         "igo": 9, "igp": 9}
+N_LOCAL = 10
 MET_Z, MET_Y, MET_ZL = 0, 1, 2
 FAR_FIRST = (4, 3, 5, 2, 6, 1, 7)
 
@@ -77,7 +77,7 @@
     kg_v, tab_v, w_v, m1_v, m2_v, mo_v, gl_v,
     u_all, ap, ao, w_o, w_p, ig_o, ig_p, pk_send, pk_recv, pk_own,
     gp, go, gp_send, gp_recv, go_send, go_recv, gz_send, gz_recv,
-    dr_v, dr_low, dr_all, ds, with_base, ds_low, dz, dz_wide, ga_low, gg, nm_v, ng_v, mg_v, m1o_v, m2o_v, keys_v,
+    dr_v, dr_low, dr_all, ds, with_base, ds_low, dz, dz_wide, ga_low, gg,
     send_sem, recv_sem, local_sem, met,
 ):
     rep = lax.axis_index("rep")
@@ -356,15 +356,18 @@
         own_total = own_total + dz_wide[step, own_piece, :]
     mean_drift = own_total / N_REP
     moment = outer_beta * mo_v[...] + mean_drift
-    nm_v[...] = moment
-    ng_v[...] = gl_v[...] - outer_rate * (mean_drift + outer_beta * moment)
-    outs = [local("nm", nm_v, nm_out)]
-    outs[-1].start()
-    outs.append(local("ng", ng_v, ng_out))
-    outs[-1].start()
+    nm_out[...] = moment
+    ng_out[...] = gl_v[...] - outer_rate * (mean_drift + outer_beta * moment)
 
     local("m1", u_all, u_all).wait()
     gosib.wait_recv()
+    def finish_keys():
+        arrived("pk", pk_recv)
+        projected = pk_own[...]
+        for step in range(3):
+            projected = projected + pk_recv[step].astype(F32)
+        keys_out[0] = rotated_heads(projected, tables, 1.0).astype(BF16)
+
     arrived("ay", dr_all)
     gz.wait_recv()
 
@@ -384,19 +387,11 @@
         stepped = master - learning_rate * (
             moment_one / (jnp.sqrt(moment_two) + adam_epsilon) + weight_decay * master
         )
-        mg_v[rows, :] = mixing * stepped + (1.0 - mixing) * spread
-        m1o_v[rows, :] = moment_one.astype(BF16)
-        m2o_v[rows, :] = moment_two.astype(BF16)
-    for name, src, dst in (("mg", mg_v, mg_out), ("m1o", m1o_v, m1_out), ("m2o", m2o_v, m2_out)):
-        local(name, src, dst.at[0]).start()
-
-    arrived("pk", pk_recv)
-    projected = pk_own[...]
-    for step in range(3):
-        projected = projected + pk_recv[step].astype(F32)
-    keys_v[...] = rotated_heads(projected, tables, 1.0).astype(BF16)
-    outs.append(local("keys", keys_v, keys_out.at[0]))
-    outs[-1].start()
+        mg_out[0, rows, :] = mixing * stepped + (1.0 - mixing) * spread
+        m1_out[0, rows, :] = moment_one.astype(BF16)
+        m2_out[0, rows, :] = moment_two.astype(BF16)
+
+    finish_keys()
 
     arrived("igo", pk_recv)
     arrived("igp", pk_recv)
@@ -408,9 +403,6 @@
     sent("dy", dr_all)
     sent("ay", dr_all)
     local("igo", gz_send, gz_send).wait()
-    local("mg", gp, gp).wait()
-    for copy in outs:
-        copy.wait()
 
 
 def hand_over(*refs):
@@ -442,8 +434,7 @@
         vmem((N_ZL, N_Y, 8, COLS), F32), vmem((N_Y, N_ZL * 8, COLS), BF16), vmem((N_Y - 1, N_ZL * 8, COLS), BF16),
         vmem(piece, F32), vmem(piece, F32), vmem((N_ZL * 8, COLS), BF16),
         vmem((3, N_ZL * 8, COLS), BF16), vmem((3, N_ZL * 8, COLS), F32), vmem((N_ZL * 8, COLS), BF16),
-        vmem((N_Y, N_ZL * 8, COLS), BF16), vmem((8, COLS), F32), vmem((8, COLS), F32), vmem((ROWS, COLS), F32),
-        vmem((ROWS, COLS), BF16), vmem((ROWS, COLS), BF16), vmem((TOK, COLS), BF16),
+        vmem((N_Y, N_ZL * 8, COLS), BF16),
         pltpu.SemaphoreType.DMA((N_SEND,)), pltpu.SemaphoreType.DMA((N_RECV,)),
         pltpu.SemaphoreType.DMA((N_LOCAL,)), pltpu.SemaphoreType.REGULAR((3,)),
     ]
@@ -457,7 +448,7 @@
         kernel,
         out_shape=tuple(vmem(out.shape, out.dtype) for out in outs),
         in_specs=[anywhere] * 9,
-        out_specs=[anywhere] * 7,
+        out_specs=[pl.BlockSpec(memory_space=pltpu.VMEM)] * 7,
         scratch_shapes=scratch,
         compiler_params=pltpu.CompilerParams(
             collective_id=0, has_side_effects=True, vmem_limit_bytes=56 * 2**20

time: 44.9 us -> 44.6 us (level)
  no operation moved by 1% of the time
where the time goes in v6:
time: 44.6 us; the launch traced here: 44.5 us
  Pallas kernels  43.9 us (98%)
  between operations  0.64 us (1%)
    pallas_call x1, Pallas kernels, body(): pl.pallas_call(kernel, out_shape=tuple((vmem(out.shape, out.dtype) for ou...  42.4 us
    pallas_call x1, Pallas kernels, body(): pl.pallas_call(hand_over, out_shape=outs, in_specs=[anywhere] * 7, out_sp...  1.42 us

profile of v6, /device:TPU:4, one launch (start us, length us, event | category | flops | bytes accessed | tf_op | source)
XLA Modules:
  0.0 44.5 jit_solution(12389303682828823304)
XLA Ops:
  0.6 42.4 %shard_map.144 = (bf16[1,128,512]{2,1,0:T(8,128)(2,1)S(1)}, bf16[1,128,4096]{2,1,0:T(8,128)(2,1)S(1)}, f32[1,256,512]{2,1,0:T(8,128)S(1)}, bf16[1,256,512]{2,1,0...) custom-call(bf16[1,128,4096]{2,1,0:T(8,128)(2,1)} %inp.1, ...), custom_call_target="tpu_custom_call" | custom-call | tf_op jit(solution)/shard_map/pallas_call | solution.py:447
  43.1 1.4 %shard_map.145 = (bf16[1,128,512]{2,1,0:T(8,128)(2,1)}, bf16[1,128,4096]{2,1,0:T(8,128)(2,1)}, f32[1,256,512]{2,1,0:T(8,128)}, bf16[1,256,512]{2,1,0:T(8,128)(2,...) custom-call(bf16[1,128,512]{2,1,0:T(8,128)(2,1)S(1)} %get-tuple-element.14.refs_0_, ...), custom_call_target="tpu_custom_call" | custom-call | tf_op jit(solution)/shard_map/pallas_call | solution.py:460
